TPU v7x, 32 devices: a whole 2x2x4 slice. The times are simulated.
32 devices in a mesh: replica: 2 (over x), section: 4 (over y, core), shard: 4 (over z).
Axes of the slice: x: 2, y: 2, z: 4, core: 2. Of those that a mesh axis runs over, the one named last changes fastest.
Arguments:
- inputs: bfloat16 [2, 1, 128, 1024], P('replica', None, None, 'shard'), may hold values from -17 to 17
- targets: bfloat16 [2, 1, 128, 1024], P('replica', None, None, 'shard'), may hold values from -6 to 6
- weight_a: bfloat16 [2, 4, 1024, 3072], P('replica', 'section', None, 'shard'), may hold values from -6 to 6
- weight_b: bfloat16 [2, 4, 3072, 1024], P('replica', 'section', 'shard'), may hold values from -6 to 6
- moment_a: bfloat16 [2, 4, 1024, 3072], P('replica', 'section', None, 'shard'), may hold values from -3 to 3
- moment_b: bfloat16 [2, 4, 3072, 1024], P('replica', 'section', 'shard'), may hold values from -3 to 3
- routes: int32 [1, 3, 2, 2], replicated, may hold values from 0 to 1, each once within a row
- partners: int32 [4, 2, 2, 2], replicated, may hold values from 0 to 1, as said below
Outputs:
- new_weight_a: bfloat16 [2, 4, 1024, 3072], P('replica', 'section', None, 'shard')
- new_weight_b: bfloat16 [2, 4, 3072, 1024], P('replica', 'section', 'shard')
- new_moment_a: bfloat16 [2, 4, 1024, 3072], P('replica', 'section', None, 'shard')
- new_moment_b: bfloat16 [2, 4, 3072, 1024], P('replica', 'section', 'shard')
Inputs may be any that keep to these rules, and one draw needn't show every extreme that they name: Each routes[m, s, q, :] names every replica once, so each replica of section s + 1 receives exactly one block from every replica of section s. For each section s, projection t and piece k, partners[s, t, k, :] is its own inverse (the partner of the partner is the replica itself); for each s, t and replica r, partners[s, t, :, r] names every replica once, and exactly one piece pairs r with itself.
All inputs are finite; a program needn't handle non-finite values.
Results may differ from a plain program's by a relative error of at most 0.022.
Values may be sent and summed in bfloat16 or wider, within the bound.
No kernel may reach another device: no remote copies, remote signals or barrier semaphores. Data moves between devices by JAX's collectives and lax.ppermute only.
A program may use at most 128 MiB of HBM per device.

v0:
```python
import math

import jax
import jax.numpy as jnp
from jax import lax
from jax.sharding import PartitionSpec as P

epsilon = 1e-05
inner_rate = 0.5
momentum_decay = 0.9
outer_rate = 0.7


def shifted(array, axis, by):
    size = lax.axis_size(axis)
    pairs = [(i, i + by) for i in range(size) if 0 <= i + by < size]
    return lax.ppermute(array, axis, pairs)


def norm_scale(gathered):
    wide = gathered.astype(jnp.float32)
    return lax.rsqrt(jnp.mean(wide * wide, axis=1, keepdims=True) + epsilon)


def keep_slot(store, value, place, valid):
    old_value = lax.dynamic_index_in_dim(store, place, 0, keepdims=False)
    return lax.dynamic_update_index_in_dim(store, jnp.where(valid, value, old_value), place, 0)


def pair_mix(weights, moments, deltas, far_weights, far_moments, far_deltas):
    mean_weight = (weights.astype(jnp.float32) + far_weights.astype(jnp.float32)) * 0.5
    mean_moment = (moments.astype(jnp.float32) + far_moments.astype(jnp.float32)) * 0.5
    mean_delta = (deltas.astype(jnp.float32) + far_deltas.astype(jnp.float32)) * 0.5
    new_moment = momentum_decay * mean_moment + mean_delta
    new_weight = mean_weight - outer_rate * (momentum_decay * new_moment + mean_delta)
    return (new_weight.astype(jnp.bfloat16), new_moment.astype(jnp.bfloat16))


def per_device(inputs, targets, weight_a, weight_b, moment_a, moment_b, routes, partners):
    replicas = lax.axis_size("replica")
    sections = lax.axis_size("section")
    replica_id = lax.axis_index("replica")
    section_id = lax.axis_index("section")
    shard_id = lax.axis_index("shard")
    batches = inputs.shape[1]
    row_count = inputs.shape[2]
    features = inputs.shape[3]
    width = weight_a.shape[2]
    local_hidden = weight_a.shape[3]
    hidden_total = local_hidden * lax.axis_size("shard")
    scale_in = 1.0 / math.sqrt(width)
    scale_out = 1.0 / math.sqrt(hidden_total)
    weight_in = weight_a[0, 0]
    weight_out = weight_b[0, 0]
    ticks = batches + sections - 1
    group_rows = row_count // replicas
    labels = jnp.arange(replicas, dtype=jnp.int32)

    def table_row(batch_index, link):
        batch_clip = jnp.clip(batch_index, 0, batches - 1)
        link_clip = jnp.clip(link, 0, sections - 2)
        return routes[batch_clip, link_clip, replica_id]

    def by_target(destination):
        match = (destination[None, :] == labels[:, None]).astype(jnp.int32)
        return jnp.sum(labels[None, :] * match, axis=1)

    incoming = jnp.zeros((row_count, features), jnp.bfloat16)
    kept_inputs = jnp.zeros((batches, row_count, width), jnp.bfloat16)
    kept_preact = jnp.zeros((batches, row_count, local_hidden), jnp.float32)
    kept_output = jnp.zeros((batches, row_count, features), jnp.bfloat16)
    for tick_index in range(ticks):
        batch_index = tick_index - section_id
        valid = (batch_index >= 0) & (batch_index < batches)
        place = jnp.clip(batch_index, 0, batches - 1)
        own_rows = lax.dynamic_index_in_dim(inputs[0], place, 0, keepdims=False)
        current = jnp.where(section_id == 0, own_rows, incoming)
        gathered = lax.all_gather(current, "shard", axis=1, tiled=True)
        inverse_rms = norm_scale(gathered)
        normed = (gathered.astype(jnp.float32) * inverse_rms).astype(jnp.bfloat16)
        preact = jnp.dot(normed, weight_in, preferred_element_type=jnp.float32) * scale_in
        hidden = jax.nn.silu(preact).astype(jnp.bfloat16)
        term = jnp.dot(hidden, weight_out, preferred_element_type=jnp.float32) * scale_out
        total = lax.psum_scatter(
            term.astype(jnp.bfloat16), "shard", scatter_dimension=1, tiled=True
        ).astype(jnp.float32)
        output = (current.astype(jnp.float32) + total).astype(jnp.bfloat16)
        kept_inputs = keep_slot(kept_inputs, gathered, place, valid)
        kept_preact = keep_slot(kept_preact, preact, place, valid)
        kept_output = keep_slot(kept_output, output, place, valid)
        if tick_index + 1 < ticks:
            order = by_target(table_row(tick_index - section_id, section_id))
            send_grouped = jnp.take(output.reshape(replicas, group_rows, features), order, axis=0)
            send_mixed = lax.all_to_all(
                send_grouped, "replica", split_axis=0, concat_axis=0, tiled=True
            )
            incoming = shifted(send_mixed.reshape(row_count, features), "section", 1)
    section_tables = lax.dynamic_index_in_dim(partners, section_id, 0, keepdims=False)
    destination_in = section_tables[0][:, replica_id]
    destination_out = section_tables[1][:, replica_id]
    order_in = by_target(destination_in)
    order_out = by_target(destination_out)

    def arrange_in(array):
        return jnp.take(array.reshape(replicas, width // replicas, local_hidden), order_in, axis=0)

    def arrange_out(array):
        return jnp.take(array.reshape(replicas, local_hidden // replicas, width), order_out, axis=0)

    state_in = arrange_in(weight_in)
    moment_in = arrange_in(moment_a[0, 0])
    state_out = arrange_out(weight_out)
    moment_out = arrange_out(moment_b[0, 0])
    incoming = jnp.zeros((row_count, features), jnp.bfloat16)
    grad_in = jnp.zeros((width, local_hidden), jnp.float32)
    grad_out = jnp.zeros((local_hidden, width), jnp.float32)
    contract_rows = (((0,), (0,)), ((), ()))
    contract_last = (((1,), (1,)), ((), ()))
    for tick_index in range(ticks):
        batch_index = tick_index - (sections - 1 - section_id)
        valid = (batch_index >= 0) & (batch_index < batches)
        place = jnp.clip(batch_index, 0, batches - 1)
        last_output = lax.dynamic_index_in_dim(kept_output, place, 0, keepdims=False)
        goal_rows = lax.dynamic_index_in_dim(targets[0], place, 0, keepdims=False)
        own_grad = (last_output.astype(jnp.float32) - goal_rows.astype(jnp.float32)).astype(
            jnp.bfloat16
        )
        upstream = jnp.where(section_id == sections - 1, own_grad, incoming)
        upstream = jnp.where(valid, upstream, jnp.zeros_like(upstream))
        gathered_up = lax.all_gather(upstream, "shard", axis=1, tiled=True)
        gathered = lax.dynamic_index_in_dim(kept_inputs, place, 0, keepdims=False)
        preact = lax.dynamic_index_in_dim(kept_preact, place, 0, keepdims=False)
        inverse_rms = norm_scale(gathered)
        normed = (gathered.astype(jnp.float32) * inverse_rms).astype(jnp.bfloat16)
        hidden = jax.nn.silu(preact).astype(jnp.bfloat16)
        grad_out = (
            grad_out
            + lax.dot_general(
                hidden, gathered_up, contract_rows, preferred_element_type=jnp.float32
            )
            * scale_out
        )
        grad_hidden = (
            lax.dot_general(
                gathered_up, weight_out, contract_last, preferred_element_type=jnp.float32
            )
            * scale_out
        )
        gate = jax.nn.sigmoid(preact)
        grad_pre = (grad_hidden * gate * (1.0 + preact * (1.0 - gate))).astype(jnp.bfloat16)
        grad_in = (
            grad_in
            + lax.dot_general(normed, grad_pre, contract_rows, preferred_element_type=jnp.float32)
            * scale_in
        )
        term = (
            lax.dot_general(grad_pre, weight_in, contract_last, preferred_element_type=jnp.float32)
            * scale_in
        )
        total = lax.psum_scatter(
            term.astype(jnp.bfloat16), "shard", scatter_dimension=1, tiled=True
        ).astype(jnp.float32)
        exact = (
            lax.dynamic_slice_in_dim(gathered, shard_id * features, features, 1).astype(jnp.float32)
            * inverse_rms
        )
        along = lax.psum(jnp.sum(total * exact, axis=1), "shard") / width
        result = (
            upstream.astype(jnp.float32) + inverse_rms * (total - exact * along[:, None])
        ).astype(jnp.bfloat16)
        if tick_index + 1 < ticks:
            send_destination = table_row(tick_index - sections + 2 + section_id, section_id)
            grouped = result.reshape(replicas, group_rows, features)
            mixed = lax.all_to_all(grouped, "replica", split_axis=0, concat_axis=0, tiled=True)
            moved = shifted(mixed, "section", -1)
            incoming = jnp.take(moved, send_destination, axis=0).reshape(row_count, features)
    delta_in = arrange_in((inner_rate * grad_in).astype(jnp.bfloat16))
    delta_out = arrange_out((inner_rate * grad_out).astype(jnp.bfloat16))
    far_state_in, far_moment_in, far_delta_in, far_state_out, far_moment_out, far_delta_out = (
        lax.all_to_all(state_in, "replica", split_axis=0, concat_axis=0, tiled=True),
        lax.all_to_all(moment_in, "replica", split_axis=0, concat_axis=0, tiled=True),
        lax.all_to_all(delta_in, "replica", split_axis=0, concat_axis=0, tiled=True),
        lax.all_to_all(state_out, "replica", split_axis=0, concat_axis=0, tiled=True),
        lax.all_to_all(moment_out, "replica", split_axis=0, concat_axis=0, tiled=True),
        lax.all_to_all(delta_out, "replica", split_axis=0, concat_axis=0, tiled=True),
    )
    new_in, new_moment_in = pair_mix(
        state_in, moment_in, delta_in, far_state_in, far_moment_in, far_delta_in
    )
    new_out, new_moment_out = pair_mix(
        state_out, moment_out, delta_out, far_state_out, far_moment_out, far_delta_out
    )
    shape_in = (1, 1, width, local_hidden)
    shape_out = (1, 1, local_hidden, width)
    new_weight_a = jnp.take(new_in, destination_in, axis=0).reshape(shape_in)
    new_moment_a = jnp.take(new_moment_in, destination_in, axis=0).reshape(shape_in)
    new_weight_b = jnp.take(new_out, destination_out, axis=0).reshape(shape_out)
    new_moment_b = jnp.take(new_moment_out, destination_out, axis=0).reshape(shape_out)
    return (new_weight_a, new_weight_b, new_moment_a, new_moment_b)


def solution(mesh):
    placed = (
        P("replica", None, None, "shard"),
        P("replica", None, None, "shard"),
        P("replica", "section", None, "shard"),
        P("replica", "section", "shard", None),
        P("replica", "section", None, "shard"),
        P("replica", "section", "shard", None),
        P(),
        P(),
    )
    return jax.shard_map(
        per_device,
        mesh=mesh,
        in_specs=placed,
        out_specs=(
            P("replica", "section", None, "shard"),
            P("replica", "section", "shard", None),
            P("replica", "section", None, "shard"),
            P("replica", "section", "shard", None),
        ),
        check_vma=False,
    )
```

profile of v0, /device:TPU:0, one launch (start us, length us, event | category | flops | bytes accessed | tf_op | source)
XLA Modules:
  0.0 563.3 jit_solution(11893147216986363338)
XLA Ops:
  8.2 15.6 %all_gather.24 = bf16[128,1024]{1,0:T(8,128)(2,1)S(1)} all-gather(bf16[128,256]{1,0:T(8,128)(2,1)S(1)} %bitcast_select_fusion.6), channel_id=1, replica_groups=mesh['replica'=2,'section'=4,'shard'=4] {'shard'}, dimensions={1}, use_global_device_ids=true | all-gather | bytes 327680 | tf_op jit(solution)/shard_map/all_gather | solution.py:78
  28.1 21.0 %reduce-scatter.8.cloned.1.call-done = bf16[128,256]{1,0:T(8,128)(2,1)} async-done(((bf16[128,1024]{1,0:T(8,128)(2,1)}), bf16[128,256]{1,0:T(8,128)(2,1)}) %reduce-scatter.8.cloned.1.call-update) | async-done | bytes 65552 | tf_op jit(solution)/shard_map/reduce_scatter | solution.py:84
  59.4 14.5 %all_gather.25 = bf16[128,1024]{1,0:T(8,128)(2,1)S(1)} all-gather(bf16[128,256]{1,0:T(8,128)(2,1)S(1)} %bitcast_select_fusion.5), channel_id=1, replica_groups=mesh['replica'=2,'section'=4,'shard'=4] {'shard'}, dimensions={1}, use_global_device_ids=true | all-gather | bytes 327680 | tf_op jit(solution)/shard_map/all_gather | solution.py:78
  76.9 20.2 %reduce-scatter.10.cloned.1.call-done = bf16[128,256]{1,0:T(8,128)(2,1)} async-done(((bf16[128,1024]{1,0:T(8,128)(2,1)}), bf16[128,256]{1,0:T(8,128)(2,1)}) %reduce-scatter.10.cloned.1.call-update) | async-done | bytes 65552 | tf_op jit(solution)/shard_map/reduce_scatter | solution.py:84
  98.6 6.7 %all_to_all.61 = bf16[2,64,256]{2,1,0:T(8,128)(2,1)S(1)} all-to-all(bf16[2,64,256]{2,1,0:T(8,128)(2,1)S(1)} %broadcast_select_fusion.14), channel_id=1, replica_groups=mesh['replica'=2,'section'=4,'shard'=4] {'replica'}, dimensions={0} | all-to-all | bytes 131072 | tf_op jit(solution)/shard_map/all_to_all | solution.py:94
  107.6 14.5 %all_gather.26 = bf16[128,1024]{1,0:T(8,128)(2,1)S(1)} all-gather(bf16[128,256]{1,0:T(8,128)(2,1)S(1)} %bitcast_select_fusion.4), channel_id=1, replica_groups=mesh['replica'=2,'section'=4,'shard'=4] {'shard'}, dimensions={1}, use_global_device_ids=true | all-gather | bytes 327680 | tf_op jit(solution)/shard_map/all_gather | solution.py:78
  125.1 20.5 %reduce-scatter.12.cloned.1.call-done = bf16[128,256]{1,0:T(8,128)(2,1)} async-done(((bf16[128,1024]{1,0:T(8,128)(2,1)}), bf16[128,256]{1,0:T(8,128)(2,1)}) %reduce-scatter.12.cloned.1.call-update) | async-done | bytes 65552 | tf_op jit(solution)/shard_map/reduce_scatter | solution.py:84
  155.9 14.5 %all_gather.27 = bf16[128,1024]{1,0:T(8,128)(2,1)S(1)} all-gather(bf16[128,256]{1,0:T(8,128)(2,1)S(1)} %bitcast_select_fusion.3), channel_id=1, replica_groups=mesh['replica'=2,'section'=4,'shard'=4] {'shard'}, dimensions={1}, use_global_device_ids=true | all-gather | bytes 327680 | tf_op jit(solution)/shard_map/all_gather | solution.py:78
  174.2 20.5 %reduce-scatter.14.cloned.1.call-done = bf16[128,256]{1,0:T(8,128)(2,1)} async-done(((bf16[128,1024]{1,0:T(8,128)(2,1)}), bf16[128,256]{1,0:T(8,128)(2,1)}) %reduce-scatter.14.cloned.1.call-update) | async-done | bytes 65552 | tf_op jit(solution)/shard_map/reduce_scatter | solution.py:84
  195.6 13.9 %all_gather.28 = bf16[128,1024]{1,0:T(8,128)(2,1)S(1)} all-gather(bf16[128,256]{1,0:T(8,128)(2,1)S(1)} %get-tuple-element.13), channel_id=1, replica_groups=mesh['replica'=2,'section'=4,'shard'=4] {'shard'}, dimensions={1}, use_global_device_ids=true | all-gather | bytes 327680 | tf_op jit(solution)/shard_map/all_gather | solution.py:130
  213.8 17.8 %reduce-scatter.16.cloned.1.call-done = bf16[128,256]{1,0:T(8,128)(2,1)} async-done(((bf16[128,1024]{1,0:T(8,128)(2,1)}), bf16[128,256]{1,0:T(8,128)(2,1)}) %reduce-scatter.16.cloned.1.call-update) | async-done | bytes 65552 | tf_op jit(solution)/shard_map/reduce_scatter | solution.py:160
  232.6 8.8 %psum.21 = f32[128]{0:T(128)S(1)} all-reduce(f32[128]{0:T(128)S(1)} %fusion.160), channel_id=1, replica_groups=mesh['replica'=2,'section'=4,'shard'=4] {'shard'}, use_global_device_ids=true, to_apply=%region_13.16 | all-reduce | flops 128 | bytes 1024 | tf_op jit(solution)/shard_map/psum | solution.py:167
  255.2 14.2 %all_gather.29 = bf16[128,1024]{1,0:T(8,128)(2,1)S(1)} all-gather(bf16[128,256]{1,0:T(8,128)(2,1)S(1)} %fusion.176), channel_id=1, replica_groups=mesh['replica'=2,'section'=4,'shard'=4] {'shard'}, dimensions={1}, use_global_device_ids=true | all-gather | bytes 327680 | tf_op jit(solution)/shard_map/all_gather | solution.py:130
  275.4 16.2 %reduce-scatter.18.cloned.1.call-done = bf16[128,256]{1,0:T(8,128)(2,1)} async-done(((bf16[128,1024]{1,0:T(8,128)(2,1)}), bf16[128,256]{1,0:T(8,128)(2,1)}) %reduce-scatter.18.cloned.1.call-update) | async-done | bytes 65552 | tf_op jit(solution)/shard_map/reduce_scatter | solution.py:160
  293.1 9.4 %psum.22 = f32[128]{0:T(128)} all-reduce(f32[128]{0:T(128)} %fusion.164), channel_id=1, replica_groups=mesh['replica'=2,'section'=4,'shard'=4] {'shard'}, use_global_device_ids=true, to_apply=%region_16.19 | all-reduce | flops 128 | bytes 1024 | tf_op jit(solution)/shard_map/psum | solution.py:167
  320.6 14.3 %all_gather.30 = bf16[128,1024]{1,0:T(8,128)(2,1)S(1)} all-gather(bf16[128,256]{1,0:T(8,128)(2,1)S(1)} %fusion.175), channel_id=1, replica_groups=mesh['replica'=2,'section'=4,'shard'=4] {'shard'}, dimensions={1}, use_global_device_ids=true | all-gather | bytes 327680 | tf_op jit(solution)/shard_map/all_gather | solution.py:130
  343.2 14.5 %reduce-scatter.20.cloned.1.call-done = bf16[128,256]{1,0:T(8,128)(2,1)} async-done(((bf16[128,1024]{1,0:T(8,128)(2,1)}), bf16[128,256]{1,0:T(8,128)(2,1)}) %reduce-scatter.20.cloned.1.call-update) | async-done | bytes 65552 | tf_op jit(solution)/shard_map/reduce_scatter | solution.py:160
  359.2 9.4 %psum.23 = f32[128]{0:T(128)} all-reduce(f32[128]{0:T(128)} %fusion.168), channel_id=1, replica_groups=mesh['replica'=2,'section'=4,'shard'=4] {'shard'}, use_global_device_ids=true, to_apply=%region_19.22 | all-reduce | flops 128 | bytes 1024 | tf_op jit(solution)/shard_map/psum | solution.py:167
  384.5 14.5 %all_gather.31 = bf16[128,1024]{1,0:T(8,128)(2,1)S(1)} all-gather(bf16[128,256]{1,0:T(8,128)(2,1)S(1)} %fusion.174), channel_id=1, replica_groups=mesh['replica'=2,'section'=4,'shard'=4] {'shard'}, dimensions={1}, use_global_device_ids=true | all-gather | bytes 327680 | tf_op jit(solution)/shard_map/all_gather | solution.py:130
  422.4 13.9 %all-to-all-done.10 = bf16[2,384,1024]{2,1,0:T(8,128)(2,1)} async-done(((bf16[2,384,1024]{2,1,0:T(8,128)(2,1)}), bf16[2,384,1024]{2,1,0:T(8,128)(2,1)}, u32[]{:S(2)}, u32[]{:S(2)}) %all-to-all-start.10) | async-done | bytes 1572896 | tf_op jit(solution)/shard_map/all_to_all | solution.py:184
  448.0 9.9 %all-to-all-done.11 = bf16[2,384,1024]{2,1,0:T(8,128)(2,1)S(1)} async-done(((bf16[2,384,1024]{2,1,0:T(8,128)(2,1)}), bf16[2,384,1024]{2,1,0:T(8,128)(2,1)S(1)}, u32[]{:S(2)}, u32[]{:S(2)}) %all-to-all-start.11) | async-done | bytes 1572896 | tf_op jit(solution)/shard_map/all_to_all | solution.py:185
  480.8 19.4 %all_to_all.63 = bf16[2,512,768]{2,1,0:T(8,128)(2,1)} all-to-all(bf16[2,512,768]{2,1,0:T(8,128)(2,1)S(1)} %get-tuple-element.29), channel_id=1, replica_groups=mesh['replica'=2,'section'=4,'shard'=4] {'replica'}, dimensions={0} | all-to-all | bytes 3145728 | tf_op jit(solution)/shard_map/all_to_all | solution.py:180
  504.1 15.1 %all-to-all-done.1 = bf16[2,512,768]{2,1,0:T(8,128)(2,1)S(1)} async-done(((bf16[2,512,768]{2,1,0:T(8,128)(2,1)}), bf16[2,512,768]{2,1,0:T(8,128)(2,1)S(1)}, u32[]{:S(2)}, u32[]{:S(2)}) %all-to-all-start.1) | async-done | bytes 1572896 | tf_op jit(solution)/shard_map/all_to_all | solution.py:181
  525.1 7.5 %fusion.1 = (bf16[2,384,1024]{2,1,0:T(8,128)(2,1)}, bf16[2,384,1024]{2,1,0:T(8,128)(2,1)}) fusion(bf16[2,384,1024]{2,1,0:T(8,128)(2,1)} %copy-done.4, bf16[2,384,1024]{2,1,0:T(8,128)(2,1)} %get-tuple-element.25, bf16[2,384,1024]{2,1,0:T(8,128)(2,1)} %all-to-all-done.10, bf16[2,384,1024]{2,1,0:T(8,128)(2,1)S(1)} %copy-done.3, ...), kind=kLoop, calls=%fused_computation.25 | loop fusion | flops 14942208 | bytes 12582912 | tf_op jit(solution)/shard_map/convert_element_type | solution.py:36
  (226 shorter events, 201.9 us)
Async XLA Ops:
  7.2 41.9 %reduce-scatter.8.cloned.1.call-start = ((), (), s32[]{:S(2)}) async-start(), calls=%async_computation.19 | async-start | bytes 327680 | tf_op jit(solution)/shard_map/reduce_scatter | solution.py:84
  27.6 46.9 %copy-start.2 = (bf16[1,1,1024,768]{3,2,1,0:T(8,128)(2,1)S(1)}, bf16[1,1,1024,768]{3,2,1,0:T(8,128)(2,1)}, u32[]{:S(2)}) copy-start(bf16[1,1,1024,768]{3,2,1,0:T(8,128)(2,1)} %param.16) | copy-start | bytes 4718596
  27.7 69.5 %reduce-scatter.10.cloned.1.call-start = ((), (), s32[]{:S(2)}) async-start(), calls=%async_computation.20 | async-start | bytes 327680 | tf_op jit(solution)/shard_map/reduce_scatter | solution.py:84
  57.2 2.2 collective-permute-start
  76.9 68.7 %reduce-scatter.12.cloned.1.call-start = ((), (), s32[]{:S(2)}) async-start(), calls=%async_computation.21 | async-start | bytes 327680 | tf_op jit(solution)/shard_map/reduce_scatter | solution.py:84
  105.4 2.2 collective-permute-start.1
  125.0 69.6 %reduce-scatter.14.cloned.1.call-start = ((), (), s32[]{:S(2)}) async-start(), calls=%async_computation.22 | async-start | bytes 327680 | tf_op jit(solution)/shard_map/reduce_scatter | solution.py:84
  153.7 2.2 collective-permute-start.2
  174.1 57.5 %reduce-scatter.16.cloned.1.call-start = ((), (), s32[]{:S(2)}) async-start(), calls=%async_computation.23 | async-start | bytes 327680 | tf_op jit(solution)/shard_map/reduce_scatter | solution.py:160
  211.9 29.5 %copy-start.29 = (bf16[128,256]{1,0:T(8,128)(2,1)S(1)}, bf16[128,256]{1,0:T(8,128)(2,1)}, u32[]{:S(2)}) copy-start(bf16[128,256]{1,0:T(8,128)(2,1)} %copy-done.28) | copy-start | bytes 196612
  243.0 7.4 %all-to-all-start.5 = ((bf16[2,64,256]{2,1,0:T(8,128)(2,1)}), bf16[2,64,256]{2,1,0:T(8,128)(2,1)S(1)}, u32[]{:S(2)}, u32[]{:S(2)}) async-start(bf16[2,64,256]{2,1,0:T(8,128)(2,1)} %bitcast.178), calls=%async_computation.10 | async-start | bytes 131072 | tf_op jit(solution)/shard_map/all_to_all | solution.py:174
  246.3 45.3 %reduce-scatter.18.cloned.1.call-start = ((), (), s32[]{:S(2)}) async-start(), calls=%async_computation.24 | async-start | bytes 327680 | tf_op jit(solution)/shard_map/reduce_scatter | solution.py:160
  250.4 3.3 collective-permute-start.3
  274.1 38.0 %copy-start.36 = (s32[2]{0:T(128)}, s32[2]{0:T(128)S(1)}, u32[]{:S(2)}) copy-start(s32[2]{0:T(128)S(1)} %get-tuple-element.7) | copy-start | bytes 28
  304.7 7.4 %all-to-all-start.6 = ((bf16[2,64,256]{2,1,0:T(8,128)(2,1)}), bf16[2,64,256]{2,1,0:T(8,128)(2,1)S(1)}, u32[]{:S(2)}, u32[]{:S(2)}) async-start(bf16[2,64,256]{2,1,0:T(8,128)(2,1)} %bitcast.177), calls=%async_computation.12 | async-start | bytes 131072 | tf_op jit(solution)/shard_map/all_to_all | solution.py:174
  308.0 49.6 %reduce-scatter.20.cloned.1.call-start = ((), (), s32[]{:S(2)}) async-start(), calls=%async_computation.25 | async-start | bytes 327680 | tf_op jit(solution)/shard_map/reduce_scatter | solution.py:160
  312.1 6.9 %collective-permute-start.4 = (bf16[2,64,256]{2,1,0:T(8,128)(2,1)S(1)}, bf16[2,64,256]{2,1,0:T(8,128)(2,1)}, u32[]{:S(2)}, u32[]{:S(2)}) collective-permute-start(bf16[2,64,256]{2,1,0:T(8,128)(2,1)S(1)} %all-to-all-done.6), channel_id=1, source_target_pairs={{4,0},{8,4},{12,8},{5,1},{9,5},{13,9},{6,2},{10,6},{14,10},{7,3},{... | collective-permute-start | bytes 196616 | tf_op jit(solution)/shard_map/ppermute | solution.py:17
  370.9 7.4 %all-to-all-start.7 = ((bf16[2,64,256]{2,1,0:T(8,128)(2,1)}), bf16[2,64,256]{2,1,0:T(8,128)(2,1)S(1)}, u32[]{:S(2)}, u32[]{:S(2)}) async-start(bf16[2,64,256]{2,1,0:T(8,128)(2,1)} %bitcast.179), calls=%async_computation.14 | async-start | bytes 131072 | tf_op jit(solution)/shard_map/all_to_all | solution.py:174
  378.3 4.7 collective-permute-start.5
  412.6 23.7 %all-to-all-start.10 = ((bf16[2,384,1024]{2,1,0:T(8,128)(2,1)}), bf16[2,384,1024]{2,1,0:T(8,128)(2,1)}, u32[]{:S(2)}, u32[]{:S(2)}) async-start(bf16[2,384,1024]{2,1,0:T(8,128)(2,1)} %get-tuple-element.24), calls=%async_computation.17 | async-start | bytes 3145728 | tf_op jit(solution)/shard_map/all_to_all | solution.py:184
  436.3 21.6 %all-to-all-start.11 = ((bf16[2,384,1024]{2,1,0:T(8,128)(2,1)}), bf16[2,384,1024]{2,1,0:T(8,128)(2,1)S(1)}, u32[]{:S(2)}, u32[]{:S(2)}) async-start(bf16[2,384,1024]{2,1,0:T(8,128)(2,1)} %get-tuple-element.25), calls=%async_computation.18 | async-start | bytes 3145728 | tf_op jit(solution)/shard_map/all_to_all | solution.py:185
  459.1 21.7 %all-to-all-start.9 = ((bf16[2,384,1024]{2,1,0:T(8,128)(2,1)}), bf16[2,384,1024]{2,1,0:T(8,128)(2,1)}, u32[]{:S(2)}, u32[]{:S(2)}) async-start(bf16[2,384,1024]{2,1,0:T(8,128)(2,1)} %get-tuple-element.26), calls=%async_computation.16 | async-start | bytes 3145728 | tf_op jit(solution)/shard_map/all_to_all | solution.py:183
  500.2 19.0 %all-to-all-start.1 = ((bf16[2,512,768]{2,1,0:T(8,128)(2,1)}), bf16[2,512,768]{2,1,0:T(8,128)(2,1)S(1)}, u32[]{:S(2)}, u32[]{:S(2)}) async-start(bf16[2,512,768]{2,1,0:T(8,128)(2,1)} %get-tuple-element.27), calls=%async_computation.1 | async-start | bytes 3145728 | tf_op jit(solution)/shard_map/all_to_all | solution.py:181
  520.3 19.1 %all-to-all-start.8 = ((bf16[2,512,768]{2,1,0:T(8,128)(2,1)}), bf16[2,512,768]{2,1,0:T(8,128)(2,1)}, u32[]{:S(2)}, u32[]{:S(2)}) async-start(bf16[2,512,768]{2,1,0:T(8,128)(2,1)} %get-tuple-element.28), calls=%async_computation.15 | async-start | bytes 3145728 | tf_op jit(solution)/shard_map/all_to_all | solution.py:182
  (40 other events, 218.8 us)
Sparse Core Ops, SparseCore 0:
  27.8 21.1 reduce-scatter.7
  77.0 20.0 reduce-scatter.9
  125.2 20.3 reduce-scatter.11
  174.2 20.3 reduce-scatter.13
  213.4 18.1 reduce-scatter.15
  273.3 18.2 reduce-scatter.17
  338.8 18.7 reduce-scatter.19
where the time goes:
time: 566 us; the launch traced here: 563 us
  waiting for transfers between devices  185 us (33%)
  blocking collectives  183 us (32%)
  other arithmetic  50.1 us (9%)
  matrix products  47.6 us (8%)
  local copies, waits for them, and re-layouts  43.5 us (8%)
  starting transfers between devices  39.4 us (7%)
  between operations  14.8 us (3%)
    reduce_scatter x7, waiting for transfers between devices, per_device(): lax.psum_scatter(term.astype(jnp.bfloat16), 'shard', scatter_dimension=1,...  131 us
    all_gather x4, blocking collectives, per_device(): gathered = lax.all_gather(current, 'shard', axis=1, tiled=True)  59.1 us
    all_gather x4, blocking collectives, per_device(): gathered_up = lax.all_gather(upstream, 'shard', axis=1, tiled=True)  56.9 us
    psum x3, blocking collectives, per_device(): along = lax.psum(jnp.sum(total * exact, axis=1), 'shard') / width  27.6 us
    all_to_all x3, blocking collectives, per_device(): lax.all_to_all(send_grouped, 'replica', split_axis=0, concat_axis=0, tile...  20 us
    all_to_all x1, blocking collectives, per_device(): lax.all_to_all(state_in, 'replica', split_axis=0, concat_axis=0, tiled=True)  19.4 us
    dot_general x4, matrix products, per_device(): lax.dot_general(hidden, gathered_up, contract_rows, preferred_element_typ...  15.7 us
    all_to_all x1, waiting for transfers between devices, per_device(): lax.all_to_all(moment_in, 'replica', split_axis=0, concat_axis=0, tiled=T...  15.1 us
  transfers between devices with their start and end apart: 21, of which 19 were waited for; matrix products, arithmetic and copies ran while one was open for 11% of the time, Pallas kernels for 0%

commit v1 on v0

v1 whole, which is shorter than its diff:
```python
import math

import jax
import jax.numpy as jnp
from jax import lax
from jax.sharding import PartitionSpec as P

epsilon = 1e-05
inner_rate = 0.5
momentum_decay = 0.9
outer_rate = 0.7

axes = ("replica", "section", "shard")
contract_rows = (((0,), (0,)), ((), ()))
contract_last = (((1,), (1,)), ((), ()))


def norm_scale(rows):
    wide = rows.astype(jnp.float32)
    return lax.rsqrt(jnp.mean(wide * wide, axis=1, keepdims=True) + epsilon)


def dot(left, right, dims=(((1,), (0,)), ((), ()))):
    return lax.dot_general(left, right, dims, preferred_element_type=jnp.float32)


def outer_mix(weight, moment, delta):
    new_moment = momentum_decay * moment + delta
    new_weight = weight - outer_rate * (momentum_decay * new_moment + delta)
    return new_weight.astype(jnp.bfloat16), new_moment.astype(jnp.bfloat16)


def per_device(inputs, targets, weight_a, weight_b, moment_a, moment_b, routes, partners):
    replicas = lax.axis_size("replica")
    sections = lax.axis_size("section")
    shards = lax.axis_size("shard")
    replica_id = lax.axis_index("replica")
    section_id = lax.axis_index("section")
    shard_id = lax.axis_index("shard")
    row_count = inputs.shape[2]
    features = inputs.shape[3]
    width = weight_a.shape[2]
    local_hidden = weight_a.shape[3]
    assert inputs.shape[1] == 1 and shards & (shards - 1) == 0
    scale_in = 1.0 / math.sqrt(width)
    scale_out = 1.0 / math.sqrt(local_hidden * shards)
    weight_in = weight_a[0, 0]
    weight_out = weight_b[0, 0]
    piece_rows = row_count // (replicas * shards)
    own_rows = replicas * piece_rows

    def flat(replica, section, shard):
        return (replica * sections + section) * shards + shard

    def across_shards(array, offset, active):
        pairs = [
            (flat(r, s, j), flat(r, s, j ^ offset))
            for r in range(replicas)
            for s in active
            for j in range(shards)
        ]
        return lax.ppermute(array, axes, pairs)

    def across_replicas(array, offset, active, step=0):
        pairs = [
            (flat(r, s, j), flat((r + offset) % replicas, s + step, j))
            for r in range(replicas)
            for s in active
            for j in range(shards)
        ]
        return lax.ppermute(array, axes, pairs)

    def gather_rows(own, active):
        parts = [own] + [across_shards(own, d, active) for d in range(1, shards)]
        return jnp.concatenate(parts, axis=0)

    def scatter_rows(term, active):
        term = term.astype(jnp.bfloat16).reshape(shards, own_rows, width)
        total = term[0].astype(jnp.float32)
        for d in range(1, shards):
            total = total + across_shards(term[d], d, active).astype(jnp.float32)
        return total

    def in_feature_order(parts):
        stacked = jnp.stack(parts)
        order = shard_id ^ jnp.arange(shards, dtype=jnp.int32)
        return jnp.concatenate(
            [lax.dynamic_index_in_dim(stacked, order[c], 0, keepdims=False) for c in range(shards)],
            axis=1,
        )

    def split_rows(array):
        blocks = array.reshape(replicas, shards, piece_rows, array.shape[1])
        places = (replica_id - jnp.arange(replicas, dtype=jnp.int32)) % replicas
        return jnp.take(blocks, places, axis=0)

    def shard_rows(split, d):
        rows = lax.dynamic_index_in_dim(split, shard_id ^ d, 1, keepdims=False)
        return rows.reshape(own_rows, split.shape[3])

    every = range(sections)
    others = range(1, replicas)

    tables = lax.dynamic_index_in_dim(partners, section_id, 0, keepdims=False)

    def piece_of(table, offset):
        wanted = (replica_id + offset) % replicas
        return jnp.argmax(table[:, replica_id] == wanted).astype(jnp.int32)

    pieces_in = [piece_of(tables[0], e) for e in range(replicas)]
    pieces_out = [piece_of(tables[1], e) for e in range(replicas)]
    size_in = width // replicas
    size_out = local_hidden // replicas

    def piece(array, index, size, axis=0):
        return lax.dynamic_slice_in_dim(array, index * size, size, axis)

    def exchange(array, pieces, size, axis=0, active=every):
        return [
            across_replicas(piece(array, pieces[e], size, axis), e, active) for e in others
        ]

    input_parts = [inputs[0, 0]] + [across_shards(inputs[0, 0], d, [0]) for d in range(1, shards)]
    first = split_rows(in_feature_order(input_parts))
    goal_split = split_rows(targets[0, 0])
    goal_parts = [shard_rows(goal_split, 0)] + [
        across_shards(shard_rows(goal_split, d), d, [sections - 1]) for d in range(1, shards)
    ]
    goal = in_feature_order(goal_parts)

    far_weight_in = exchange(weight_in, pieces_in, size_in)
    far_moment_in = exchange(moment_a[0, 0], pieces_in, size_in)
    far_weight_out = exchange(weight_out, pieces_out, size_out)
    far_moment_out = exchange(moment_b[0, 0], pieces_out, size_out)

    def slots(link):
        table = routes[0, link, replica_id]
        labels = jnp.arange(replicas, dtype=jnp.int32)
        return jnp.sum(
            labels[None, :] * (table[None, :] == labels[:, None]).astype(jnp.int32), axis=1
        )

    rows = jnp.concatenate([shard_rows(first, d) for d in range(shards)], axis=0)
    for step in range(sections):
        if step > 0:
            rows = jnp.where(section_id == step, gather_rows(incoming, [step]), rows)
        own = rows[:own_rows]
        inverse_rms = norm_scale(rows)
        normed = (rows.astype(jnp.float32) * inverse_rms).astype(jnp.bfloat16)
        preact = dot(normed, weight_in) * scale_in
        hidden = jax.nn.silu(preact).astype(jnp.bfloat16)
        total = scatter_rows(dot(hidden, weight_out) * scale_out, [step])
        output = (own.astype(jnp.float32) + total).astype(jnp.bfloat16)
        if step + 1 < sections:
            blocks = output.reshape(replicas, piece_rows, width)
            order = slots(step)
            received = []
            for e in range(replicas):
                block = order[(replica_id + e) % replicas]
                place = (replica_id - block) % replicas
                chosen = lax.dynamic_index_in_dim(blocks, place, 0, keepdims=False)
                received.append(across_replicas(chosen, e, [step], 1))
            incoming = jnp.concatenate(received, axis=0)

    far_normed = exchange(normed, pieces_in, size_in, 1)
    far_hidden = exchange(hidden, pieces_out, size_out, 1)

    gate = jax.nn.sigmoid(preact)
    slope = gate * (1.0 + preact * (1.0 - gate))
    own_scale = inverse_rms[:own_rows]
    exact = own.astype(jnp.float32) * own_scale
    incoming = (output.astype(jnp.float32) - goal.astype(jnp.float32)).astype(jnp.bfloat16)
    upstream = jnp.zeros((row_count, width), jnp.bfloat16)
    far_up = [jnp.zeros((row_count, width), jnp.bfloat16) for _ in others]
    far_pre = [jnp.zeros((row_count, local_hidden), jnp.bfloat16) for _ in others]
    for step in reversed(range(sections)):
        here = section_id == step
        upstream = jnp.where(here, gather_rows(incoming, [step]), upstream)
        far_up = [
            jnp.where(here, across_replicas(upstream, e, [step]), far_up[e - 1]) for e in others
        ]
        grad_hidden = dot(upstream, weight_out, contract_last) * scale_out
        grad_pre = (grad_hidden * slope).astype(jnp.bfloat16)
        far_pre = [
            jnp.where(here, across_replicas(grad_pre, e, [step]), far_pre[e - 1]) for e in others
        ]
        if step > 0:
            total = scatter_rows(dot(grad_pre, weight_in, contract_last) * scale_in, [step])
            along = jnp.mean(total * exact, axis=1, keepdims=True)
            result = (
                upstream[:own_rows].astype(jnp.float32) + own_scale * (total - exact * along)
            ).astype(jnp.bfloat16)
            blocks = result.reshape(replicas, piece_rows, width)
            received = jnp.stack(
                [across_replicas(blocks[e], -e, [step], -1) for e in range(replicas)]
            )
            table = routes[0, step - 1, replica_id]
            placed = []
            for e in range(replicas):
                sender = table[(replica_id - e) % replicas]
                placed.append(
                    lax.dynamic_index_in_dim(
                        received, (sender - replica_id) % replicas, 0, keepdims=False
                    )
                )
            incoming = jnp.concatenate(placed, axis=0)

    def as_delta(left, right, scale):
        return (inner_rate * (dot(left, right, contract_rows) * scale)).astype(jnp.bfloat16)

    def finish(weight, moment, left, right, far_weights, far_moments, far_left, far_right, scale,
               pieces, size):
        new_weight, new_moment = outer_mix(
            weight.astype(jnp.float32),
            moment.astype(jnp.float32),
            as_delta(left, right, scale).astype(jnp.float32),
        )
        for e in others:
            back = replicas - e

            def mean(own_array, far_array):
                return 0.5 * (own_array.astype(jnp.float32) + far_array.astype(jnp.float32))

            index = pieces[back]
            own_left = piece(left, index, size, 1)
            part_weight, part_moment = outer_mix(
                mean(piece(weight, index, size), far_weights[e - 1]),
                mean(piece(moment, index, size), far_moments[e - 1]),
                mean(
                    as_delta(own_left, right, scale),
                    as_delta(far_left[e - 1], far_right[e - 1], scale),
                ),
            )
            new_weight = lax.dynamic_update_slice_in_dim(new_weight, part_weight, index * size, 0)
            new_moment = lax.dynamic_update_slice_in_dim(new_moment, part_moment, index * size, 0)
        return new_weight[None, None], new_moment[None, None]

    new_weight_b, new_moment_b = finish(
        weight_out, moment_b[0, 0], hidden, upstream, far_weight_out, far_moment_out,
        far_hidden, far_up, scale_out, pieces_out, size_out,
    )
    new_weight_a, new_moment_a = finish(
        weight_in, moment_a[0, 0], normed, grad_pre, far_weight_in, far_moment_in,
        far_normed, far_pre, scale_in, pieces_in, size_in,
    )
    return (new_weight_a, new_weight_b, new_moment_a, new_moment_b)


def solution(mesh):
    placed = (
        P("replica", None, None, "shard"),
        P("replica", None, None, "shard"),
        P("replica", "section", None, "shard"),
        P("replica", "section", "shard", None),
        P("replica", "section", None, "shard"),
        P("replica", "section", "shard", None),
        P(),
        P(),
    )
    return jax.shard_map(
        per_device,
        mesh=mesh,
        in_specs=placed,
        out_specs=(
            P("replica", "section", None, "shard"),
            P("replica", "section", "shard", None),
            P("replica", "section", None, "shard"),
            P("replica", "section", "shard", None),
        ),
        check_vma=False,
    )
```

time: 566 us -> 346 us (0.61)
  blocking collectives: 183 us -> 0 us
  starting transfers between devices: 39.4 us -> 84.9 us
  other arithmetic: 50.1 us -> 15.9 us
  matrix products: 47.6 us -> 16.9 us
  local copies, waits for them, and re-layouts: 43.5 us -> 29.9 us
  waiting for transfers between devices: 185 us -> 176 us
    ppermute x6 -> x74, waiting for transfers between devices: 3.9 us -> 176 us  [the longest x26 158 us: across_replicas(): return lax.ppermute(array, axes, pairs)]
    reduce_scatter x7 -> x0, waiting for transfers between devices: 131 us -> none  [per_device(): lax.psum_scatter(term.astype(jnp.bfloat16), 'shard', scatter_dimension=1,...]
    all_gather x8 -> x0, blocking collectives: 116 us -> none  [the longest x4 59.1 us: per_device(): gathered = lax.all_gather(current, 'shard', axis=1, tiled=True)]
    ppermute x6 -> x74, starting transfers between devices: 7.69 us -> 84.9 us  [the longest x48 59.1 us: across_shards(): return lax.ppermute(array, axes, pairs)]
    all_to_all x8 -> x0, waiting for transfers between devices: 50.3 us -> none  [the longest x1 15.1 us: per_device(): lax.all_to_all(moment_in, 'replica', split_axis=0, concat_axis=0, tiled=T...]
    all_to_all x4 -> x0, blocking collectives: 39.4 us -> none  [the longest x3 20 us: per_device(): lax.all_to_all(send_grouped, 'replica', split_axis=0, concat_axis=0, tile...]
    gather x16 -> x2, local copies, waits for them, and re-layouts: 34 us -> 2.06 us  [split_rows(): return jnp.take(blocks, places, axis=0)]
    all_to_all x8 -> x0, starting transfers between devices: 31.5 us -> none  [the longest x3 9.89 us: per_device(): lax.all_to_all(grouped, 'replica', split_axis=0, concat_axis=0, tiled=True)]
  transfers between devices with their start and end apart: 21 -> 74, of which waited for: 19 -> 11; matrix products, arithmetic and copies ran while one was open for 11% -> 8% of each run, Pallas kernels for 0% -> 0%
where the time goes in v1:
time: 346 us; the launch traced here: 343 us
  waiting for transfers between devices  176 us (51%)
  starting transfers between devices  84.9 us (25%)
  local copies, waits for them, and re-layouts  29.9 us (9%)
  between operations  19.5 us (6%)
  matrix products  16.9 us (5%)
  other arithmetic  15.9 us (5%)
    ppermute x26, waiting for transfers between devices, across_replicas(): return lax.ppermute(array, axes, pairs)  158 us
    ppermute x48, starting transfers between devices, across_shards(): return lax.ppermute(array, axes, pairs)  59.1 us
    ppermute x26, starting transfers between devices, across_replicas(): return lax.ppermute(array, axes, pairs)  25.9 us
    ppermute x48, waiting for transfers between devices, across_shards(): return lax.ppermute(array, axes, pairs)  18.8 us
    dot_general x18, matrix products, dot(): lax.dot_general(left, right, dims, preferred_element_type=jnp.float32)  16.9 us
    unnamed x101, local copies, waits for them, and re-layouts  8.35 us
  transfers between devices with their start and end apart: 74, of which 11 were waited for; matrix products, arithmetic and copies ran while one was open for 8% of the time, Pallas kernels for 0%

profile of v1, /device:TPU:0, one launch (start us, length us, event | category | flops | bytes accessed | tf_op | source)
XLA Modules:
  0.0 343.5 jit_solution(1526591967726401906)
XLA Ops:
  0.6 5.1 %collective-permute-start = (bf16[128,256]{1,0:T(8,128)(2,1)}, bf16[128,256]{1,0:T(8,128)(2,1)S(1)}, u32[]{:S(2)}, u32[]{:S(2)}) collective-permute-start(bf16[128,256]{1,0:T(8,128)(2,1)} %bitcast.307), channel_id=1, source_target_pairs={{0,1},{1,0},{2,3},{3,2},{16,17},{17,16},{18,19},{19,18}} | collective-permute-start | bytes 196616 | tf_op jit(solution)/shard_map/ppermute | solution.py:62
  5.7 4.5 %collective-permute-start.1 = (bf16[128,256]{1,0:T(8,128)(2,1)}, bf16[128,256]{1,0:T(8,128)(2,1)S(1)}, u32[]{:S(2)}, u32[]{:S(2)}) collective-permute-start(bf16[128,256]{1,0:T(8,128)(2,1)} %bitcast.308), channel_id=1, source_target_pairs={{0,2},{1,3},{2,0},{3,1},{16,18},{17,19},{18,16},{19,17}} | collective-permute-start | bytes 196616 | tf_op jit(solution)/shard_map/ppermute | solution.py:62
  10.2 1.9 collective-permute-start.2
  25.9 1.6 fusion.74
  29.0 2.8 collective-permute-start.3
  31.8 5.4 %collective-permute-start.4 = (bf16[32,1024]{1,0:T(8,128)(2,1)}, bf16[32,1024]{1,0:T(8,128)(2,1)S(1)}, u32[]{:S(2)}, u32[]{:S(2)}) collective-permute-start(bf16[32,1024]{1,0:T(8,128)(2,1)} %get-tuple-element.59), channel_id=1, source_target_pairs={{0,2},{1,3},{2,0},{3,1},{16,18},{17,19},{18,16},{19,17}} | collective-permute-start | bytes 196616 | tf_op jit(solution)/shard_map/ppermute | solution.py:62
  37.2 1.9 collective-permute-start.5
  42.0 3.2 collective-permute-done.5
  55.9 1.6 fusion.71
  73.6 1.6 fusion.68
  143.2 135.4 %collective-permute-done.55 = bf16[16,1024]{1,0:T(8,128)(2,1)S(1)} collective-permute-done((bf16[16,1024]{1,0:T(8,128)(2,1)S(1)}, bf16[16,1024]{1,0:T(8,128)(2,1)S(1)}, u32[]{:S(2)}, u32[]{:S(2)}) %collective-permute-start.55) | collective-permute-done | bytes 32800 | tf_op jit(solution)/shard_map/ppermute | solution.py:71
  280.0 9.0 %collective-permute-done.56 = bf16[16,1024]{1,0:T(8,128)(2,1)S(1)} collective-permute-done((bf16[16,1024]{1,0:T(8,128)(2,1)S(1)}, bf16[16,1024]{1,0:T(8,128)(2,1)S(1)}, u32[]{:S(2)}, u32[]{:S(2)}) %collective-permute-start.56) | collective-permute-done | bytes 32800 | tf_op jit(solution)/shard_map/ppermute | solution.py:71
  289.1 1.9 collective-permute-start.57
  291.1 4.2 %collective-permute-done.57 = bf16[32,1024]{1,0:T(8,128)(2,1)S(1)} collective-permute-done((bf16[32,1024]{1,0:T(8,128)(2,1)S(1)}, bf16[32,1024]{1,0:T(8,128)(2,1)S(1)}, u32[]{:S(2)}, u32[]{:S(2)}) %collective-permute-start.57) | collective-permute-done | bytes 65568 | tf_op jit(solution)/shard_map/ppermute | solution.py:62
  295.3 1.9 collective-permute-start.58
  297.2 5.3 %collective-permute-done.58 = bf16[32,1024]{1,0:T(8,128)(2,1)S(1)} collective-permute-done((bf16[32,1024]{1,0:T(8,128)(2,1)S(1)}, bf16[32,1024]{1,0:T(8,128)(2,1)S(1)}, u32[]{:S(2)}, u32[]{:S(2)}) %collective-permute-start.58) | collective-permute-done | bytes 65568 | tf_op jit(solution)/shard_map/ppermute | solution.py:62
  302.5 1.9 collective-permute-start.59
  304.4 6.0 %collective-permute-done.59 = bf16[32,1024]{1,0:T(8,128)(2,1)S(1)} collective-permute-done((bf16[32,1024]{1,0:T(8,128)(2,1)S(1)}, bf16[32,1024]{1,0:T(8,128)(2,1)S(1)}, u32[]{:S(2)}, u32[]{:S(2)}) %collective-permute-start.59) | collective-permute-done | bytes 65568 | tf_op jit(solution)/shard_map/ppermute | solution.py:62
  317.2 4.3 %collective-permute-done.62 = bf16[128,512]{1,0:T(8,128)(2,1)S(1)} collective-permute-done((bf16[128,512]{1,0:T(8,128)(2,1)S(1)}, bf16[128,512]{1,0:T(8,128)(2,1)S(1)}, u32[]{:S(2)}, u32[]{:S(2)}) %collective-permute-start.62) | collective-permute-done | bytes 131104 | tf_op jit(solution)/shard_map/ppermute | solution.py:71
  323.5 2.8 collective-permute-start.63
  328.8 2.2 collective-permute-done.63
  331.1 2.8 collective-permute-start.70
  335.1 4.3 %collective-permute-done.70 = bf16[128,1024]{1,0:T(8,128)(2,1)S(1)} collective-permute-done((bf16[128,1024]{1,0:T(8,128)(2,1)S(1)}, bf16[128,1024]{1,0:T(8,128)(2,1)S(1)}, u32[]{:S(2)}, u32[]{:S(2)}) %collective-permute-start.70) | collective-permute-done | bytes 262176 | tf_op jit(solution)/shard_map/ppermute | solution.py:71
  339.3 2.5 fusion.135
  (332 shorter events, 109.9 us)
Async XLA Ops:
  0.6 21.6 %collective-permute-start = (bf16[128,256]{1,0:T(8,128)(2,1)}, bf16[128,256]{1,0:T(8,128)(2,1)S(1)}, u32[]{:S(2)}, u32[]{:S(2)}) collective-permute-start(bf16[128,256]{1,0:T(8,128)(2,1)} %bitcast.307), channel_id=1, source_target_pairs={{0,1},{1,0},{2,3},{3,2},{16,17},{17,16},{18,19},{19,18}} | collective-permute-start | bytes 196616 | tf_op jit(solution)/shard_map/ppermute | solution.py:62
  5.7 16.5 %collective-permute-start.1 = (bf16[128,256]{1,0:T(8,128)(2,1)}, bf16[128,256]{1,0:T(8,128)(2,1)S(1)}, u32[]{:S(2)}, u32[]{:S(2)}) collective-permute-start(bf16[128,256]{1,0:T(8,128)(2,1)} %bitcast.308), channel_id=1, source_target_pairs={{0,2},{1,3},{2,0},{3,1},{16,18},{17,19},{18,16},{19,17}} | collective-permute-start | bytes 196616 | tf_op jit(solution)/shard_map/ppermute | solution.py:62
  10.2 12.0 %collective-permute-start.2 = (bf16[128,256]{1,0:T(8,128)(2,1)}, bf16[128,256]{1,0:T(8,128)(2,1)S(1)}, u32[]{:S(2)}, u32[]{:S(2)}) collective-permute-start(bf16[128,256]{1,0:T(8,128)(2,1)} %bitcast.309), channel_id=1, source_target_pairs={{0,3},{1,2},{2,1},{3,0},{16,19},{17,18},{18,17},{19,16}} | collective-permute-start | bytes 196616 | tf_op jit(solution)/shard_map/ppermute | solution.py:62
  29.0 12.9 %collective-permute-start.3 = (bf16[32,1024]{1,0:T(8,128)(2,1)}, bf16[32,1024]{1,0:T(8,128)(2,1)S(1)}, u32[]{:S(2)}, u32[]{:S(2)}) collective-permute-start(bf16[32,1024]{1,0:T(8,128)(2,1)} %get-tuple-element.57), channel_id=1, source_target_pairs={{0,1},{1,0},{2,3},{3,2},{16,17},{17,16},{18,19},{19,18}} | collective-permute-start | bytes 196616 | tf_op jit(solution)/shard_map/ppermute | solution.py:62
  31.8 10.1 %collective-permute-start.4 = (bf16[32,1024]{1,0:T(8,128)(2,1)}, bf16[32,1024]{1,0:T(8,128)(2,1)S(1)}, u32[]{:S(2)}, u32[]{:S(2)}) collective-permute-start(bf16[32,1024]{1,0:T(8,128)(2,1)} %get-tuple-element.59), channel_id=1, source_target_pairs={{0,2},{1,3},{2,0},{3,1},{16,18},{17,19},{18,16},{19,17}} | collective-permute-start | bytes 196616 | tf_op jit(solution)/shard_map/ppermute | solution.py:62
  37.2 8.0 %collective-permute-start.5 = (bf16[32,1024]{1,0:T(8,128)(2,1)S(1)}, bf16[32,1024]{1,0:T(8,128)(2,1)S(1)}, u32[]{:S(2)}, u32[]{:S(2)}) collective-permute-start(bf16[32,1024]{1,0:T(8,128)(2,1)S(1)} %get-tuple-element.58), channel_id=1, source_target_pairs={{0,3},{1,2},{2,1},{3,0},{16,19},{17,18},{18,17},{19,16}} | collective-permute-start | bytes 196616 | tf_op jit(solution)/shard_map/ppermute | solution.py:62
  76.7 5.9 %collective-permute-start.19 = (bf16[32,1024]{1,0:T(8,128)(2,1)}, bf16[32,1024]{1,0:T(8,128)(2,1)}, u32[]{:S(2)}, u32[]{:S(2)}) collective-permute-start(bf16[32,1024]{1,0:T(8,128)(2,1)} %get-tuple-element.51), channel_id=1, source_target_pairs={{8,9},{9,8},{10,11},{11,10},{24,25},{25,24},{26,27},{27,26}} | collective-permute-start | bytes 196616 | tf_op jit(solution)/shard_map/ppermute | solution.py:62
  111.5 210.6 %collective-permute-start.67 = (bf16[384,1024]{1,0:T(8,128)(2,1)}, bf16[384,1024]{1,0:T(8,128)(2,1)}, u32[]{:S(2)}, u32[]{:S(2)}) collective-permute-start(bf16[384,1024]{1,0:T(8,128)(2,1)} %dynamic-slice_bitcast_fusion.1), channel_id=1, source_target_pairs={{0,16},{1,17},{2,18},{3,19},{4,20},{5,21},{6,22},{7,23},{8,24},{9,... | collective-permute-start | bytes 2359304 | tf_op jit(solution)/shard_map/ppermute | solution.py:71
  118.8 216.2 %collective-permute-start.68 = (bf16[384,1024]{1,0:T(8,128)(2,1)}, bf16[384,1024]{1,0:T(8,128)(2,1)}, u32[]{:S(2)}, u32[]{:S(2)}) collective-permute-start(bf16[384,1024]{1,0:T(8,128)(2,1)} %dynamic-slice_bitcast_fusion), channel_id=1, source_target_pairs={{0,16},{1,17},{2,18},{3,19},{4,20},{5,21},{6,22},{7,23},{8,24},{9,... | collective-permute-start | bytes 2359304 | tf_op jit(solution)/shard_map/ppermute | solution.py:71
  130.4 5.5 %collective-permute-start.52 = (bf16[32,1024]{1,0:T(8,128)(2,1)}, bf16[32,1024]{1,0:T(8,128)(2,1)S(1)}, u32[]{:S(2)}, u32[]{:S(2)}) collective-permute-start(bf16[32,1024]{1,0:T(8,128)(2,1)} %get-tuple-element.39), channel_id=1, source_target_pairs={{4,5},{5,4},{6,7},{7,6},{20,21},{21,20},{22,23},{23,22}} | collective-permute-start | bytes 196616 | tf_op jit(solution)/shard_map/ppermute | solution.py:62
  131.1 6.4 %collective-permute-start.53 = (bf16[32,1024]{1,0:T(8,128)(2,1)}, bf16[32,1024]{1,0:T(8,128)(2,1)}, u32[]{:S(2)}, u32[]{:S(2)}) collective-permute-start(bf16[32,1024]{1,0:T(8,128)(2,1)} %get-tuple-element.41), channel_id=1, source_target_pairs={{4,6},{5,7},{6,4},{7,5},{20,22},{21,23},{22,20},{23,21}} | collective-permute-start | bytes 196616 | tf_op jit(solution)/shard_map/ppermute | solution.py:62
  135.9 186.9 %collective-permute-start.60 = (bf16[512,768]{1,0:T(8,128)(2,1)}, bf16[512,768]{1,0:T(8,128)(2,1)S(1)}, u32[]{:S(2)}, u32[]{:S(2)}) collective-permute-start(bf16[512,768]{1,0:T(8,128)(2,1)} %dynamic-slice_bitcast_fusion.3), channel_id=1, source_target_pairs={{0,16},{1,17},{2,18},{3,19},{4,20},{5,21},{6,22},{7,23},{8,24},{9,... | collective-permute-start | bytes 2359304 | tf_op jit(solution)/shard_map/ppermute | solution.py:71
  139.6 138.9 %collective-permute-start.55 = (bf16[16,1024]{1,0:T(8,128)(2,1)S(1)}, bf16[16,1024]{1,0:T(8,128)(2,1)S(1)}, u32[]{:S(2)}, u32[]{:S(2)}) collective-permute-start(bf16[16,1024]{1,0:T(8,128)(2,1)S(1)} %get-tuple-element.68), channel_id=1, source_target_pairs={{4,0},{5,1},{6,2},{7,3},{20,16},{21,17},{22,18},{23,19}} | collective-permute-start | bytes 98312 | tf_op jit(solution)/shard_map/ppermute | solution.py:71
  140.9 148.1 %collective-permute-start.56 = (bf16[16,1024]{1,0:T(8,128)(2,1)S(1)}, bf16[16,1024]{1,0:T(8,128)(2,1)S(1)}, u32[]{:S(2)}, u32[]{:S(2)}) collective-permute-start(bf16[16,1024]{1,0:T(8,128)(2,1)S(1)} %get-tuple-element.69), channel_id=1, source_target_pairs={{4,16},{5,17},{6,18},{7,19},{20,0},{21,1},{22,2},{23,3}} | collective-permute-start | bytes 98312 | tf_op jit(solution)/shard_map/ppermute | solution.py:71
  278.6 45.0 %collective-permute-start.61 = (bf16[512,768]{1,0:T(8,128)(2,1)}, bf16[512,768]{1,0:T(8,128)(2,1)S(1)}, u32[]{:S(2)}, u32[]{:S(2)}) collective-permute-start(bf16[512,768]{1,0:T(8,128)(2,1)} %dynamic-slice_bitcast_fusion.2), channel_id=1, source_target_pairs={{0,16},{1,17},{2,18},{3,19},{4,20},{5,21},{6,22},{7,23},{8,24},{9,... | collective-permute-start | bytes 2359304 | tf_op jit(solution)/shard_map/ppermute | solution.py:71
  289.1 6.2 %collective-permute-start.57 = (bf16[32,1024]{1,0:T(8,128)(2,1)S(1)}, bf16[32,1024]{1,0:T(8,128)(2,1)S(1)}, u32[]{:S(2)}, u32[]{:S(2)}) collective-permute-start(bf16[32,1024]{1,0:T(8,128)(2,1)S(1)} %pad_maximum_fusion.6), channel_id=1, source_target_pairs={{0,1},{1,0},{2,3},{3,2},{16,17},{17,16},{18,19},{19,18}} | collective-permute-start | bytes 196616 | tf_op jit(solution)/shard_map/ppermute | solution.py:62
  295.3 7.2 %collective-permute-start.58 = (bf16[32,1024]{1,0:T(8,128)(2,1)S(1)}, bf16[32,1024]{1,0:T(8,128)(2,1)S(1)}, u32[]{:S(2)}, u32[]{:S(2)}) collective-permute-start(bf16[32,1024]{1,0:T(8,128)(2,1)S(1)} %pad_maximum_fusion.6), channel_id=1, source_target_pairs={{0,2},{1,3},{2,0},{3,1},{16,18},{17,19},{18,16},{19,17}} | collective-permute-start | bytes 196616 | tf_op jit(solution)/shard_map/ppermute | solution.py:62
  302.5 7.9 %collective-permute-start.59 = (bf16[32,1024]{1,0:T(8,128)(2,1)S(1)}, bf16[32,1024]{1,0:T(8,128)(2,1)S(1)}, u32[]{:S(2)}, u32[]{:S(2)}) collective-permute-start(bf16[32,1024]{1,0:T(8,128)(2,1)S(1)} %pad_maximum_fusion.6), channel_id=1, source_target_pairs={{0,3},{1,2},{2,1},{3,0},{16,19},{17,18},{18,17},{19,16}} | collective-permute-start | bytes 196616 | tf_op jit(solution)/shard_map/ppermute | solution.py:62
  310.5 5.6 %collective-permute-start.69 = (bf16[128,384]{1,0:T(8,128)(2,1)S(1)}, bf16[128,384]{1,0:T(8,128)(2,1)S(1)}, u32[]{:S(2)}, u32[]{:S(2)}) collective-permute-start(bf16[128,384]{1,0:T(8,128)(2,1)S(1)} %constant_dynamic-slice_fusion), channel_id=1, source_target_pairs={{0,16},{1,17},{2,18},{3,19},{4,20},{5,21},{6,22},{7,23},{8,24},{9,... | collective-permute-start | bytes 294920 | tf_op jit(solution)/shard_map/ppermute | solution.py:71
  323.5 7.6 %collective-permute-start.63 = (bf16[128,768]{1,0:T(8,128)(2,1)S(1)}, bf16[128,768]{1,0:T(8,128)(2,1)S(1)}, u32[]{:S(2)}, u32[]{:S(2)}) collective-permute-start(bf16[128,768]{1,0:T(8,128)(2,1)S(1)} %fusion.122), channel_id=1, source_target_pairs={{0,16},{1,17},{2,18},{3,19},{16,0},{17,1},{18,2},{19,3}} | collective-permute-start | bytes 589832 | tf_op jit(solution)/shard_map/ppermute | solution.py:71
  326.8 8.3 %collective-permute-start.73 = (bf16[128,1024]{1,0:T(8,128)(2,1)S(1)}, bf16[128,1024]{1,0:T(8,128)(2,1)S(1)}, u32[]{:S(2)}, u32[]{:S(2)}) collective-permute-start(bf16[128,1024]{1,0:T(8,128)(2,1)S(1)} %copy-done.5), channel_id=1, source_target_pairs={{12,28},{13,29},{14,30},{15,31},{28,12},{29,13},{30,14},{31,15}} | collective-permute-start | bytes 786440 | tf_op jit(solution)/shard_map/ppermute | solution.py:71
  327.5 7.6 %collective-permute-start.72 = (bf16[128,1024]{1,0:T(8,128)(2,1)S(1)}, bf16[128,1024]{1,0:T(8,128)(2,1)S(1)}, u32[]{:S(2)}, u32[]{:S(2)}) collective-permute-start(bf16[128,1024]{1,0:T(8,128)(2,1)S(1)} %copy-done.10), channel_id=1, source_target_pairs={{8,24},{9,25},{10,26},{11,27},{24,8},{25,9},{26,10},{27,11}} | collective-permute-start | bytes 786440 | tf_op jit(solution)/shard_map/ppermute | solution.py:71
  328.2 6.9 %collective-permute-start.71 = (bf16[128,1024]{1,0:T(8,128)(2,1)S(1)}, bf16[128,1024]{1,0:T(8,128)(2,1)S(1)}, u32[]{:S(2)}, u32[]{:S(2)}) collective-permute-start(bf16[128,1024]{1,0:T(8,128)(2,1)S(1)} %copy-done.12), channel_id=1, source_target_pairs={{4,20},{5,21},{6,22},{7,23},{20,4},{21,5},{22,6},{23,7}} | collective-permute-start | bytes 786440 | tf_op jit(solution)/shard_map/ppermute | solution.py:71
  331.1 8.3 %collective-permute-start.70 = (bf16[128,1024]{1,0:T(8,128)(2,1)S(1)}, bf16[128,1024]{1,0:T(8,128)(2,1)S(1)}, u32[]{:S(2)}, u32[]{:S(2)}) collective-permute-start(bf16[128,1024]{1,0:T(8,128)(2,1)S(1)} %broadcast_select_fusion.1), channel_id=1, source_target_pairs={{0,16},{1,17},{2,18},{3,19},{16,0},{17,1},{18,2},{19,3}} | collective-permute-start | bytes 786440 | tf_op jit(solution)/shard_map/ppermute | solution.py:71
  (93 other events, 884.0 us)

commit v2 on v1

v2 whole, which is shorter than its diff:
```python
import math

import jax
import jax.numpy as jnp
from jax import lax
from jax.sharding import PartitionSpec as P

epsilon = 1e-05
inner_rate = 0.5
momentum_decay = 0.9
outer_rate = 0.7

axes = ("replica", "section", "shard")
contract_rows = (((0,), (0,)), ((), ()))
contract_last = (((1,), (1,)), ((), ()))


def norm_scale(rows):
    wide = rows.astype(jnp.float32)
    return lax.rsqrt(jnp.mean(wide * wide, axis=1, keepdims=True) + epsilon)


def dot(left, right, dims=(((1,), (0,)), ((), ()))):
    return lax.dot_general(left, right, dims, preferred_element_type=jnp.float32)


def outer_mix(weight, moment, delta):
    new_moment = momentum_decay * moment + delta
    new_weight = weight - outer_rate * (momentum_decay * new_moment + delta)
    return new_weight.astype(jnp.bfloat16), new_moment.astype(jnp.bfloat16)


def per_device(inputs, targets, weight_a, weight_b, moment_a, moment_b, routes, partners):
    replicas = lax.axis_size("replica")
    sections = lax.axis_size("section")
    shards = lax.axis_size("shard")
    replica_id = lax.axis_index("replica")
    section_id = lax.axis_index("section")
    shard_id = lax.axis_index("shard")
    row_count = inputs.shape[2]
    features = inputs.shape[3]
    width = weight_a.shape[2]
    local_hidden = weight_a.shape[3]
    assert inputs.shape[1] == 1 and shards & (shards - 1) == 0
    scale_in = 1.0 / math.sqrt(width)
    scale_out = 1.0 / math.sqrt(local_hidden * shards)
    weight_in = weight_a[0, 0]
    weight_out = weight_b[0, 0]
    block_rows = row_count // replicas
    half = shards // 2

    def flat(replica, section, shard):
        return (replica * sections + section) * shards + shard

    def holder(section):
        return half - 1 + ((section ^ (section >> 1)) & 1)

    def move(array, sources, target):
        pairs = [
            (flat(r, s, j), flat(*target(r, s, j)))
            for r in range(replicas)
            for s, j in sources
        ]
        return lax.ppermute(array, axes, pairs)

    def to_holder(array, offset, active):
        return move(array, [(s, holder(s) ^ offset) for s in active], lambda r, s, j: (r, s, j ^ offset))

    def from_holder(array, offset, active):
        return move(array, [(s, holder(s)) for s in active], lambda r, s, j: (r, s, j ^ offset))

    def between_holders(array, offset, section, step):
        return move(
            array,
            [(section, holder(section))],
            lambda r, s, j: ((r + offset) % replicas, s + step, holder(s + step)),
        )

    def across_replicas(array, offset, active):
        return move(
            array,
            [(s, j) for s in active for j in range(shards)],
            lambda r, s, j: ((r + offset) % replicas, s, j),
        )

    def gather_features(array, section):
        parts = [array] + [to_holder(array, d, [section]) for d in range(1, shards)]
        return jnp.concatenate([parts[c ^ holder(section)] for c in range(shards)], axis=1)

    def by_offset(array):
        places = (replica_id - jnp.arange(replicas, dtype=jnp.int32)) % replicas
        blocks = array.reshape(replicas, block_rows, array.shape[1])
        return jnp.take(blocks, places, axis=0).reshape(array.shape)

    every = range(sections)
    others = range(1, replicas)
    is_holder = shard_id == half - 1 + ((section_id ^ (section_id >> 1)) & 1)

    def broadcast(array, active):
        total = from_holder(array, 1, active)
        for d in range(2, shards):
            total = total + from_holder(array, d, active)
        return jnp.where(is_holder, array, total)

    tables = lax.dynamic_index_in_dim(partners, section_id, 0, keepdims=False)

    def piece_of(table, offset):
        wanted = (replica_id + offset) % replicas
        return jnp.argmax(table[:, replica_id] == wanted).astype(jnp.int32)

    pieces_in = [piece_of(tables[0], e) for e in range(replicas)]
    pieces_out = [piece_of(tables[1], e) for e in range(replicas)]
    size_in = width // replicas
    size_out = local_hidden // replicas

    def piece(array, index, size, axis=0):
        return lax.dynamic_slice_in_dim(array, index * size, size, axis)

    def exchange_state(weight, moment, pieces, size):
        return [
            across_replicas(
                jnp.concatenate([piece(weight, pieces[e], size), piece(moment, pieces[e], size)]),
                e,
                every,
            )
            for e in others
        ]

    def exchange_factor(array, pieces, size):
        return [across_replicas(piece(array, pieces[e], size, 1), e, every) for e in others]

    parts_in = [weight_in] + [to_holder(weight_in, d, every) for d in range(1, shards)]
    parts_out = [weight_out] + [to_holder(weight_out, d, every) for d in range(1, shards)]
    far_state_in = exchange_state(weight_in, moment_a[0, 0], pieces_in, size_in)
    far_state_out = exchange_state(weight_out, moment_b[0, 0], pieces_out, size_out)
    rows = by_offset(gather_features(inputs[0, 0], 0))
    goal = by_offset(gather_features(targets[0, 0], sections - 1))
    rows, goal, far_state_in, far_state_out = lax.optimization_barrier(
        (rows, goal, far_state_in, far_state_out)
    )

    def slots(link):
        table = routes[0, link, replica_id]
        labels = jnp.arange(replicas, dtype=jnp.int32)
        return jnp.sum(
            labels[None, :] * (table[None, :] == labels[:, None]).astype(jnp.int32), axis=1
        )

    def normalise(rows):
        inverse_rms = norm_scale(rows)
        return inverse_rms, (rows.astype(jnp.float32) * inverse_rms).astype(jnp.bfloat16)

    def slope_of(preact):
        gate = jax.nn.sigmoid(preact)
        return gate * (1.0 + preact * (1.0 - gate))

    for step in range(sections):
        if step > 0:
            rows = jnp.where(section_id == step, incoming, rows)
        inverse_rms, normed = normalise(rows)
        preacts = [dot(normed, part) * scale_in for part in parts_in]
        output = rows.astype(jnp.float32)
        for preact, part in zip(preacts, parts_out):
            hidden = jax.nn.silu(preact).astype(jnp.bfloat16)
            term = (dot(hidden, part) * scale_out).astype(jnp.bfloat16)
            output = output + term.astype(jnp.float32)
        output = output.astype(jnp.bfloat16)
        if step + 1 < sections:
            blocks = output.reshape(replicas, block_rows, width)
            order = slots(step)
            received = []
            for e in range(replicas):
                block = order[(replica_id + e) % replicas]
                place = (replica_id - block) % replicas
                chosen = lax.dynamic_index_in_dim(blocks, place, 0, keepdims=False)
                received.append(between_holders(chosen, e, step, 1))
            incoming = jnp.concatenate(received, axis=0)

    slopes = [slope_of(preact) for preact in preacts]
    exact = rows.astype(jnp.float32) * inverse_rms
    own_rows = broadcast(rows, every)
    normed = normalise(own_rows)[1]
    preact = dot(normed, weight_in) * scale_in
    hidden = jax.nn.silu(preact).astype(jnp.bfloat16)
    slope = slope_of(preact)
    far_normed = exchange_factor(normed, pieces_in, size_in)
    far_hidden = exchange_factor(hidden, pieces_out, size_out)

    incoming = (output.astype(jnp.float32) - goal.astype(jnp.float32)).astype(jnp.bfloat16)
    upstream = jnp.zeros((row_count, width), jnp.bfloat16)
    for step in reversed(range(sections)):
        upstream = jnp.where(section_id == step, incoming, upstream)
        if step > 0:
            total = jnp.zeros((row_count, width), jnp.float32)
            for local_slope, part_in, part_out in zip(slopes, parts_in, parts_out):
                grad_hidden = dot(upstream, part_out, contract_last) * scale_out
                grad_pre = (grad_hidden * local_slope).astype(jnp.bfloat16)
                term = (dot(grad_pre, part_in, contract_last) * scale_in).astype(jnp.bfloat16)
                total = total + term.astype(jnp.float32)
            along = jnp.mean(total * exact, axis=1, keepdims=True)
            result = (
                upstream.astype(jnp.float32) + inverse_rms * (total - exact * along)
            ).astype(jnp.bfloat16)
            blocks = result.reshape(replicas, block_rows, width)
            received = jnp.stack(
                [between_holders(blocks[e], -e, step, -1) for e in range(replicas)]
            )
            table = routes[0, step - 1, replica_id]
            placed = []
            for e in range(replicas):
                sender = table[(replica_id - e) % replicas]
                placed.append(
                    lax.dynamic_index_in_dim(
                        received, (sender - replica_id) % replicas, 0, keepdims=False
                    )
                )
            incoming = jnp.concatenate(placed, axis=0)
            if step == 2:
                incoming, normed, hidden, slope, far_normed, far_hidden = lax.optimization_barrier(
                    (incoming, normed, hidden, slope, far_normed, far_hidden)
                )

    upstream = broadcast(upstream, every)
    far_up = [across_replicas(upstream, e, every) for e in others]
    grad_hidden = dot(upstream, weight_out, contract_last) * scale_out
    grad_pre = (grad_hidden * slope).astype(jnp.bfloat16)
    far_pre = [across_replicas(grad_pre, e, every) for e in others]

    def as_delta(left, right, scale):
        return (inner_rate * (dot(left, right, contract_rows) * scale)).astype(jnp.bfloat16)

    def finish(weight, moment, left, right, far_state, far_left, far_right, scale, pieces, size):
        new_weight, new_moment = outer_mix(
            weight.astype(jnp.float32),
            moment.astype(jnp.float32),
            as_delta(left, right, scale).astype(jnp.float32),
        )
        for e in others:
            back = replicas - e

            def mean(own_array, far_array):
                return 0.5 * (own_array.astype(jnp.float32) + far_array.astype(jnp.float32))

            index = pieces[back]
            own_left = piece(left, index, size, 1)
            part_weight, part_moment = outer_mix(
                mean(piece(weight, index, size), far_state[e - 1][:size]),
                mean(piece(moment, index, size), far_state[e - 1][size:]),
                mean(
                    as_delta(own_left, right, scale),
                    as_delta(far_left[e - 1], far_right[e - 1], scale),
                ),
            )
            new_weight = lax.dynamic_update_slice_in_dim(new_weight, part_weight, index * size, 0)
            new_moment = lax.dynamic_update_slice_in_dim(new_moment, part_moment, index * size, 0)
        return new_weight[None, None], new_moment[None, None]

    new_weight_b, new_moment_b = finish(
        weight_out, moment_b[0, 0], hidden, upstream, far_state_out, far_hidden, far_up,
        scale_out, pieces_out, size_out,
    )
    new_weight_a, new_moment_a = finish(
        weight_in, moment_a[0, 0], normed, grad_pre, far_state_in, far_normed, far_pre,
        scale_in, pieces_in, size_in,
    )
    return (new_weight_a, new_weight_b, new_moment_a, new_moment_b)


def solution(mesh):
    placed = (
        P("replica", None, None, "shard"),
        P("replica", None, None, "shard"),
        P("replica", "section", None, "shard"),
        P("replica", "section", "shard", None),
        P("replica", "section", None, "shard"),
        P("replica", "section", "shard", None),
        P(),
        P(),
    )
    return jax.shard_map(
        per_device,
        mesh=mesh,
        in_specs=placed,
        out_specs=(
            P("replica", "section", None, "shard"),
            P("replica", "section", "shard", None),
            P("replica", "section", None, "shard"),
            P("replica", "section", "shard", None),
        ),
        check_vma=False,
    )
```

time: 346 us -> 326 us (0.942)
  matrix products: 16.9 us -> 118 us
  waiting for transfers between devices: 176 us -> 81.9 us
  local copies, waits for them, and re-layouts: 29.9 us -> 16.1 us
  between operations: 19.5 us -> 10.9 us
  starting transfers between devices: 84.9 us -> 78.1 us
    dot_general x18 -> x40, matrix products: 16.9 us -> 118 us  [dot(): lax.dot_general(left, right, dims, preferred_element_type=jnp.float32)]
    ppermute x74 -> x36, waiting for transfers between devices: 176 us -> 81.9 us  [move(): return lax.ppermute(array, axes, pairs)]
    ppermute x74 -> x36, starting transfers between devices: 84.9 us -> 78.1 us  [move(): return lax.ppermute(array, axes, pairs)]
    slice x8 -> x0, local copies, waits for them, and re-layouts: 6.67 us -> none  [the longest x7 6.08 us: scatter_rows(): total = total + across_shards(term[d], d, active).astype(jnp.float32)]
    unnamed x101 -> x72, local copies, waits for them, and re-layouts: 8.35 us -> 2.96 us
    squeeze x3, local copies, waits for them, and re-layouts: 0.04 us -> 3.65 us  [per_device(): chosen = lax.dynamic_index_in_dim(blocks, place, 0, keepdims=False)]
  transfers between devices with their start and end apart: 74 -> 36, of which waited for: 11 -> 7; matrix products, arithmetic and copies ran while one was open for 8% -> 19% of each run, Pallas kernels for 0% -> 0%
where the time goes in v2:
time: 326 us; the launch traced here: 324 us
  matrix products  118 us (36%)
  waiting for transfers between devices  81.9 us (25%)
  starting transfers between devices  78.1 us (24%)
  other arithmetic  18.6 us (6%)
  local copies, waits for them, and re-layouts  16.1 us (5%)
  between operations  10.9 us (3%)
    dot_general x40, matrix products, dot(): lax.dot_general(left, right, dims, preferred_element_type=jnp.float32)  118 us
    ppermute x36, waiting for transfers between devices, move(): return lax.ppermute(array, axes, pairs)  81.9 us
    ppermute x36, starting transfers between devices, move(): return lax.ppermute(array, axes, pairs)  78.1 us
  transfers between devices with their start and end apart: 36, of which 7 were waited for; matrix products, arithmetic and copies ran while one was open for 19% of the time, Pallas kernels for 0%

profile of v2, /device:TPU:0, one launch (start us, length us, event | category | flops | bytes accessed | tf_op | source)
XLA Modules:
  0.0 323.9 jit_solution(3195552475389269983)
XLA Ops:
  19.5 37.6 %collective-permute-start = (bf16[128,256]{1,0:T(8,128)(2,1)S(1)}, bf16[128,256]{1,0:T(8,128)(2,1)S(1)}, u32[]{:S(2)}, u32[]{:S(2)}) collective-permute-start(bf16[128,256]{1,0:T(8,128)(2,1)S(1)} %bitcast.249), channel_id=1, source_target_pairs={{0,1},{16,17}} | collective-permute-start | bytes 196616 | tf_op jit(solution)/shard_map/ppermute | solution.py:64
  65.4 12.5 %collective-permute-done.7 = bf16[768,1024]{1,0:T(8,128)(2,1)} collective-permute-done((bf16[768,1024]{1,0:T(8,128)(2,1)S(1)}, bf16[768,1024]{1,0:T(8,128)(2,1)}, u32[]{:S(2)}, u32[]{:S(2)}) %collective-permute-start.7) | collective-permute-done | bytes 1572896 | tf_op jit(solution)/shard_map/ppermute | solution.py:64
  77.9 3.8 %collective-permute-start.9 = (bf16[768,1024]{1,0:T(8,128)(2,1)}, bf16[768,1024]{1,0:T(8,128)(2,1)S(1)}, u32[]{:S(2)}, u32[]{:S(2)}) collective-permute-start(bf16[768,1024]{1,0:T(8,128)(2,1)} %bitcast.18), channel_id=1, source_target_pairs={{0,1},{7,6},{11,10},{12,13},{16,17},{23,22},{27,26},{28,29}} | collective-permute-start | bytes 4718600 | tf_op jit(solution)/shard_map/ppermute | solution.py:64
  99.9 16.9 %collective-permute-done.8 = bf16[1024,768]{1,0:T(8,128)(2,1)S(1)} collective-permute-done((bf16[1024,768]{1,0:T(8,128)(2,1)}, bf16[1024,768]{1,0:T(8,128)(2,1)S(1)}, u32[]{:S(2)}, u32[]{:S(2)}) %collective-permute-start.8) | collective-permute-done | bytes 1572896 | tf_op jit(solution)/shard_map/ppermute | solution.py:64
  118.4 3.9 %fusion.20 = bf16[128,1024]{1,0:T(8,128)(2,1)} fusion(f32[128,1024]{1,0:T(8,128)} %fusion.26, f32[128,1024]{1,0:T(8,128)} %fusion.24, f32[128,1024]{1,0:T(8,128)} %fusion.22, bf16[128,1024]{1,0:T(8,128)(2,1)S(1)} %bitcast.231, bf16[1,1,768,1024]{3,2,1,0:T(8,128)(2,1)} %param.13, bf16[1,1,1024,768]{3,2,1,0:T(8,128)(2,1)} %param.12, f32[128]{0:T(128)S(1)} %add_rsqrt_fusion.4), kind=kOutput, calls=%fused_computation.68 | convolution fusion | flops 404815872 | bytes 5243392 | tf_op jit(solution)/shard_map/dot_general | solution.py:24
  129.6 3.7 %fusion.39 = f32[128,1024]{1,0:T(8,128)} fusion(bf16[768,1024]{1,0:T(8,128)(2,1)} %collective-permute-done.13, bf16[1024,768]{1,0:T(8,128)(2,1)} %collective-permute-done.12, bf16[128,1024]{1,0:T(8,128)(2,1)} %get-tuple-element.41, f32[128]{0:T(128)S(1)} %add_rsqrt_fusion.3), kind=kOutput, calls=%fused_computation.87 | convolution fusion | flops 404029440 | bytes 3932672 | tf_op jit(solution)/shard_map/dot_general | solution.py:24
  138.6 3.9 %fusion.33 = bf16[128,1024]{1,0:T(8,128)(2,1)} fusion(f32[128,1024]{1,0:T(8,128)} %fusion.39, f32[128,1024]{1,0:T(8,128)} %fusion.37, f32[128,1024]{1,0:T(8,128)} %fusion.35, bf16[128,1024]{1,0:T(8,128)(2,1)S(1)} %copy-done.6, bf16[1,1,768,1024]{3,2,1,0:T(8,128)(2,1)} %param.13, bf16[1,1,1024,768]{3,2,1,0:T(8,128)(2,1)} %param.12, f32[128]{0:T(128)S(1)} %add_rsqrt_fusion.3), kind=kOutput, calls=%fused_computation.81 | convolution fusion | flops 404815872 | bytes 5243392 | tf_op jit(solution)/shard_map/dot_general | solution.py:24
  148.7 3.7 %fusion.52 = f32[128,1024]{1,0:T(8,128)} fusion(bf16[768,1024]{1,0:T(8,128)(2,1)} %collective-permute-done.13, bf16[1024,768]{1,0:T(8,128)(2,1)} %collective-permute-done.12, bf16[128,1024]{1,0:T(8,128)(2,1)S(1)} %get-tuple-element.39, f32[128]{0:T(128)S(1)} %add_rsqrt_fusion.2), kind=kOutput, calls=%fused_computation.100 | convolution fusion | flops 404029440 | bytes 3932672 | tf_op jit(solution)/shard_map/dot_general | solution.py:24
  157.6 3.9 %fusion.46 = bf16[128,1024]{1,0:T(8,128)(2,1)} fusion(f32[128,1024]{1,0:T(8,128)} %fusion.52, f32[128,1024]{1,0:T(8,128)} %fusion.50, f32[128,1024]{1,0:T(8,128)} %fusion.48, bf16[128,1024]{1,0:T(8,128)(2,1)S(1)} %get-tuple-element.39, bf16[1,1,768,1024]{3,2,1,0:T(8,128)(2,1)} %param.13, bf16[1,1,1024,768]{3,2,1,0:T(8,128)(2,1)} %param.12, ...), kind=kOutput, calls=%fused_computation.94 | convolution fusion | flops 404815872 | bytes 5243392 | tf_op jit(solution)/shard_map/dot_general | solution.py:24
  186.6 4.2 %fusion.69 = f32[128,1024]{1,0:T(8,128)} fusion(bf16[128,1024]{1,0:T(8,128)(2,1)} %fusion.128, bf16[1,1,768,1024]{3,2,1,0:T(8,128)(2,1)} %param.13, bf16[1,1,1024,768]{3,2,1,0:T(8,128)(2,1)} %param.12, f32[128,768]{1,0:T(8,128)} %copy-done.13), kind=kOutput, calls=%fused_computation.117 | convolution fusion | flops 404029440 | bytes 4325376 | tf_op jit(solution)/shard_map/dot_general | solution.py:24
  190.8 4.2 %fusion.78 = f32[128,1024]{1,0:T(8,128)} fusion(bf16[1024,768]{1,0:T(8,128)(2,1)} %collective-permute-done.12, bf16[128,1024]{1,0:T(8,128)(2,1)} %fusion.128, bf16[768,1024]{1,0:T(8,128)(2,1)} %collective-permute-done.13, f32[128,768]{1,0:T(8,128)} %copy-done.12), kind=kOutput, calls=%fused_computation.126 | convolution fusion | flops 404029440 | bytes 4325376 | tf_op jit(solution)/shard_map/dot_general | solution.py:24
  195.0 4.2 %fusion.76 = f32[128,1024]{1,0:T(8,128)} fusion(bf16[1024,768]{1,0:T(8,128)(2,1)} %collective-permute-done.10, bf16[128,1024]{1,0:T(8,128)(2,1)} %fusion.128, bf16[768,1024]{1,0:T(8,128)(2,1)} %collective-permute-done.11, f32[128,768]{1,0:T(8,128)} %copy-done.11), kind=kOutput, calls=%fused_computation.124 | convolution fusion | flops 404029440 | bytes 4325376 | tf_op jit(solution)/shard_map/dot_general | solution.py:24
  199.2 3.7 %fusion.74 = f32[128,1024]{1,0:T(8,128)} fusion(f32[128,1024]{1,0:T(8,128)} %fusion.78, f32[128,1024]{1,0:T(8,128)} %fusion.76, f32[128,1024]{1,0:T(8,128)} %fusion.69, bf16[1024,768]{1,0:T(8,128)(2,1)S(1)} %collective-permute-done.8, bf16[128,1024]{1,0:T(8,128)(2,1)} %fusion.128, bf16[768,1024]{1,0:T(8,128)(2,1)S(1)} %collective-permute-done.9, ...), kind=kOutput, calls=%fused_computation.122 | convolution fusion | flops 404422656 | bytes 5898240 | tf_op jit(solution)/shard_map/dot_general | solution.py:24
  210.4 4.2 %fusion.80 = f32[128,1024]{1,0:T(8,128)} fusion(bf16[128,1024]{1,0:T(8,128)(2,1)} %maximum_select_fusion.3, bf16[1,1,768,1024]{3,2,1,0:T(8,128)(2,1)} %param.13, bf16[1,1,1024,768]{3,2,1,0:T(8,128)(2,1)} %param.12, f32[128,768]{1,0:T(8,128)} %copy-done.13), kind=kOutput, calls=%fused_computation.128 | convolution fusion | flops 404029440 | bytes 4325376 | tf_op jit(solution)/shard_map/dot_general | solution.py:24
  214.6 4.2 %fusion.89 = f32[128,1024]{1,0:T(8,128)} fusion(bf16[1024,768]{1,0:T(8,128)(2,1)} %collective-permute-done.12, bf16[128,1024]{1,0:T(8,128)(2,1)} %maximum_select_fusion.3, bf16[768,1024]{1,0:T(8,128)(2,1)} %collective-permute-done.13, f32[128,768]{1,0:T(8,128)} %copy-done.12), kind=kOutput, calls=%fused_computation.137 | convolution fusion | flops 404029440 | bytes 4325376 | tf_op jit(solution)/shard_map/dot_general | solution.py:24
  218.8 4.2 %fusion.87 = f32[128,1024]{1,0:T(8,128)} fusion(bf16[1024,768]{1,0:T(8,128)(2,1)} %collective-permute-done.10, bf16[128,1024]{1,0:T(8,128)(2,1)} %maximum_select_fusion.3, bf16[768,1024]{1,0:T(8,128)(2,1)} %collective-permute-done.11, f32[128,768]{1,0:T(8,128)} %copy-done.11), kind=kOutput, calls=%fused_computation.135 | convolution fusion | flops 404029440 | bytes 4325376 | tf_op jit(solution)/shard_map/dot_general | solution.py:24
  223.0 3.7 %fusion.153 = (f32[128]{0:T(128)S(1)}, f32[128,1024]{1,0:T(8,128)}) fusion(bf16[128,1024]{1,0:T(8,128)(2,1)S(1)} %get-tuple-element.37, f32[128]{0:T(128)S(1)} %add_rsqrt_fusion.1, f32[128,1024]{1,0:T(8,128)} %fusion.89, f32[128,1024]{1,0:T(8,128)} %fusion.87, f32[128,1024]{1,0:T(8,128)} %fusion.80, bf16[1024,768]{1,0:T(8,128)(2,1)S(1)} %collective-permute-done.8, ...), kind=kOutput, calls=%fused_computation.247 | convolution fusion | flops 404946816 | bytes 6161408 | tf_op jit(solution)/shard_map/dot_general | solution.py:24
  231.9 5.5 %collective-permute-done.28 = bf16[128,384]{1,0:T(8,128)(2,1)S(1)} collective-permute-done((bf16[128,384]{1,0:T(8,128)(2,1)S(1)}, bf16[128,384]{1,0:T(8,128)(2,1)S(1)}, u32[]{:S(2)}, u32[]{:S(2)}) %collective-permute-start.28) | collective-permute-done | bytes 98336 | tf_op jit(solution)/shard_map/ppermute | solution.py:64
  238.8 4.2 %fusion.91 = f32[128,1024]{1,0:T(8,128)} fusion(bf16[128,1024]{1,0:T(8,128)(2,1)} %broadcast_select_fusion.2, bf16[1,1,768,1024]{3,2,1,0:T(8,128)(2,1)} %param.13, bf16[1,1,1024,768]{3,2,1,0:T(8,128)(2,1)} %param.12, f32[128,768]{1,0:T(8,128)} %copy-done.13), kind=kOutput, calls=%fused_computation.139 | convolution fusion | flops 404029440 | bytes 4325376 | tf_op jit(solution)/shard_map/dot_general | solution.py:24
  243.0 4.2 %fusion.100 = f32[128,1024]{1,0:T(8,128)} fusion(bf16[1024,768]{1,0:T(8,128)(2,1)} %collective-permute-done.12, bf16[128,1024]{1,0:T(8,128)(2,1)} %broadcast_select_fusion.2, bf16[768,1024]{1,0:T(8,128)(2,1)} %collective-permute-done.13, f32[128,768]{1,0:T(8,128)} %copy-done.12), kind=kOutput, calls=%fused_computation.148 | convolution fusion | flops 404029440 | bytes 4325376 | tf_op jit(solution)/shard_map/dot_general | solution.py:24
  247.2 4.2 %fusion.98 = f32[128,1024]{1,0:T(8,128)} fusion(bf16[1024,768]{1,0:T(8,128)(2,1)} %collective-permute-done.10, bf16[128,1024]{1,0:T(8,128)(2,1)} %broadcast_select_fusion.2, bf16[768,1024]{1,0:T(8,128)(2,1)} %collective-permute-done.11, f32[128,768]{1,0:T(8,128)} %copy-done.11), kind=kOutput, calls=%fused_computation.146 | convolution fusion | flops 404029440 | bytes 4325376 | tf_op jit(solution)/shard_map/dot_general | solution.py:24
  251.4 3.7 %fusion.158 = (f32[128]{0:T(128)S(1)}, f32[128,1024]{1,0:T(8,128)}) fusion(bf16[128,1024]{1,0:T(8,128)(2,1)S(1)} %get-tuple-element.37, f32[128]{0:T(128)S(1)} %add_rsqrt_fusion.1, f32[128,1024]{1,0:T(8,128)} %fusion.100, f32[128,1024]{1,0:T(8,128)} %fusion.98, f32[128,1024]{1,0:T(8,128)} %fusion.91, bf16[1024,768]{1,0:T(8,128)(2,1)S(1)} %collective-permute-done.8, ...), kind=kOutput, calls=%fused_computation.252 | convolution fusion | flops 404946816 | bytes 6161408 | tf_op jit(solution)/shard_map/dot_general | solution.py:24
  262.4 40.9 %collective-permute-done.31 = bf16[128,1024]{1,0:T(8,128)(2,1)S(1)} collective-permute-done((bf16[128,1024]{1,0:T(8,128)(2,1)S(1)}, bf16[128,1024]{1,0:T(8,128)(2,1)S(1)}, u32[]{:S(2)}, u32[]{:S(2)}) %collective-permute-start.31) | collective-permute-done | bytes 262176 | tf_op jit(solution)/shard_map/ppermute | solution.py:64
  318.4 3.8 %fusion.130 = (bf16[1,1,768,1024]{3,2,1,0:T(8,128)(2,1)S(1)}, bf16[1,1,768,1024]{3,2,1,0:T(8,128)(2,1)S(1)}) fusion(bf16[1,1,768,1024]{3,2,1,0:T(8,128)(2,1)S(1)} %get-tuple-element.46, s32[]{:T(128)S(6)} %select_n.257, bf16[768,1024]{1,0:T(8,128)(2,1)} %collective-permute-done.7, bf16[1,1,768,1024]{3,2,1,0:T(8,128)(2,1)S(1)} %copy-done.16, ...), kind=kOutput, calls=%fused_computation.208 | convolution fusion | flops 108920832 | bytes 5865476 | tf_op jit(solution)/shard_map/dot_general | solution.py:24
  (217 shorter events, 124.0 us)
Async XLA Ops:
  6.5 54.9 %collective-permute-start.6 = (bf16[1024,768]{1,0:T(8,128)(2,1)}, bf16[1024,768]{1,0:T(8,128)(2,1)}, u32[]{:S(2)}, u32[]{:S(2)}) collective-permute-start(bf16[1024,768]{1,0:T(8,128)(2,1)} %pad_maximum_fusion), channel_id=1, source_target_pairs={{0,16},{1,17},{2,18},{3,19},{4,20},{5,21},{6,22},{7,23},{8,24},{9,... | collective-permute-start | bytes 4718600 | tf_op jit(solution)/shard_map/ppermute | solution.py:64
  12.2 65.7 %collective-permute-start.7 = (bf16[768,1024]{1,0:T(8,128)(2,1)S(1)}, bf16[768,1024]{1,0:T(8,128)(2,1)}, u32[]{:S(2)}, u32[]{:S(2)}) collective-permute-start(bf16[768,1024]{1,0:T(8,128)(2,1)S(1)} %pad_maximum_fusion.1), channel_id=1, source_target_pairs={{0,16},{1,17},{2,18},{3,19},{4,20},{5,21},{6,22},{7,23},{8,24},{9,... | collective-permute-start | bytes 4718600 | tf_op jit(solution)/shard_map/ppermute | solution.py:64
  12.3 69.4 %collective-permute-start.13 = (bf16[768,1024]{1,0:T(8,128)(2,1)}, bf16[768,1024]{1,0:T(8,128)(2,1)}, u32[]{:S(2)}, u32[]{:S(2)}) collective-permute-start(bf16[768,1024]{1,0:T(8,128)(2,1)} %bitcast.18), channel_id=1, source_target_pairs={{2,1},{5,6},{9,10},{14,13},{18,17},{21,22},{25,26},{30,29}} | collective-permute-start | bytes 4718600 | tf_op jit(solution)/shard_map/ppermute | solution.py:64
  15.5 74.1 %collective-permute-start.12 = (bf16[1024,768]{1,0:T(8,128)(2,1)}, bf16[1024,768]{1,0:T(8,128)(2,1)}, u32[]{:S(2)}, u32[]{:S(2)}) collective-permute-start(bf16[1024,768]{1,0:T(8,128)(2,1)} %bitcast), channel_id=1, source_target_pairs={{2,1},{5,6},{9,10},{14,13},{18,17},{21,22},{25,26},{30,29}} | collective-permute-start | bytes 4718600 | tf_op jit(solution)/shard_map/ppermute | solution.py:64
  19.5 40.1 %collective-permute-start = (bf16[128,256]{1,0:T(8,128)(2,1)S(1)}, bf16[128,256]{1,0:T(8,128)(2,1)S(1)}, u32[]{:S(2)}, u32[]{:S(2)}) collective-permute-start(bf16[128,256]{1,0:T(8,128)(2,1)S(1)} %bitcast.249), channel_id=1, source_target_pairs={{0,1},{16,17}} | collective-permute-start | bytes 196616 | tf_op jit(solution)/shard_map/ppermute | solution.py:64
  59.6 33.6 %collective-permute-start.11 = (bf16[768,1024]{1,0:T(8,128)(2,1)}, bf16[768,1024]{1,0:T(8,128)(2,1)}, u32[]{:S(2)}, u32[]{:S(2)}) collective-permute-start(bf16[768,1024]{1,0:T(8,128)(2,1)} %bitcast.18), channel_id=1, source_target_pairs={{3,1},{4,6},{8,10},{15,13},{19,17},{20,22},{24,26},{31,29}} | collective-permute-start | bytes 4718600 | tf_op jit(solution)/shard_map/ppermute | solution.py:64
  61.4 31.8 %collective-permute-start.10 = (bf16[1024,768]{1,0:T(8,128)(2,1)}, bf16[1024,768]{1,0:T(8,128)(2,1)}, u32[]{:S(2)}, u32[]{:S(2)}) collective-permute-start(bf16[1024,768]{1,0:T(8,128)(2,1)} %bitcast), channel_id=1, source_target_pairs={{3,1},{4,6},{8,10},{15,13},{19,17},{20,22},{24,26},{31,29}} | collective-permute-start | bytes 4718600 | tf_op jit(solution)/shard_map/ppermute | solution.py:64
  77.9 22.0 %collective-permute-start.9 = (bf16[768,1024]{1,0:T(8,128)(2,1)}, bf16[768,1024]{1,0:T(8,128)(2,1)S(1)}, u32[]{:S(2)}, u32[]{:S(2)}) collective-permute-start(bf16[768,1024]{1,0:T(8,128)(2,1)} %bitcast.18), channel_id=1, source_target_pairs={{0,1},{7,6},{11,10},{12,13},{16,17},{23,22},{27,26},{28,29}} | collective-permute-start | bytes 4718600 | tf_op jit(solution)/shard_map/ppermute | solution.py:64
  81.7 35.0 %collective-permute-start.8 = (bf16[1024,768]{1,0:T(8,128)(2,1)}, bf16[1024,768]{1,0:T(8,128)(2,1)S(1)}, u32[]{:S(2)}, u32[]{:S(2)}) collective-permute-start(bf16[1024,768]{1,0:T(8,128)(2,1)} %bitcast), channel_id=1, source_target_pairs={{0,1},{7,6},{11,10},{12,13},{16,17},{23,22},{27,26},{28,29}} | collective-permute-start | bytes 4718600 | tf_op jit(solution)/shard_map/ppermute | solution.py:64
  124.0 3.9 %collective-permute-start.15 = (bf16[64,1024]{1,0:T(8,128)(2,1)}, bf16[64,1024]{1,0:T(8,128)(2,1)S(1)}, u32[]{:S(2)}, u32[]{:S(2)}) collective-permute-start(bf16[64,1024]{1,0:T(8,128)(2,1)} %get-tuple-element.70), channel_id=1, source_target_pairs={{1,22},{17,6}} | collective-permute-start | bytes 393224 | tf_op jit(solution)/shard_map/ppermute | solution.py:64
  143.5 4.0 %collective-permute-start.17 = (bf16[64,1024]{1,0:T(8,128)(2,1)S(1)}, bf16[64,1024]{1,0:T(8,128)(2,1)S(1)}, u32[]{:S(2)}, u32[]{:S(2)}) collective-permute-start(bf16[64,1024]{1,0:T(8,128)(2,1)S(1)} %get-tuple-element.68), channel_id=1, source_target_pairs={{6,26},{22,10}} | collective-permute-start | bytes 393224 | tf_op jit(solution)/shard_map/ppermute | solution.py:64
  162.5 5.4 %collective-permute-start.19 = (bf16[64,1024]{1,0:T(8,128)(2,1)S(1)}, bf16[64,1024]{1,0:T(8,128)(2,1)S(1)}, u32[]{:S(2)}, u32[]{:S(2)}) collective-permute-start(bf16[64,1024]{1,0:T(8,128)(2,1)S(1)} %get-tuple-element.66), channel_id=1, source_target_pairs={{10,29},{26,13}} | collective-permute-start | bytes 393224 | tf_op jit(solution)/shard_map/ppermute | solution.py:64
  163.2 4.7 %collective-permute-start.18 = (bf16[64,1024]{1,0:T(8,128)(2,1)S(1)}, bf16[64,1024]{1,0:T(8,128)(2,1)}, u32[]{:S(2)}, u32[]{:S(2)}) collective-permute-start(bf16[64,1024]{1,0:T(8,128)(2,1)S(1)} %get-tuple-element.65), channel_id=1, source_target_pairs={{10,13},{26,29}} | collective-permute-start | bytes 393224 | tf_op jit(solution)/shard_map/ppermute | solution.py:64
  169.1 33.9 %collective-permute-start.26 = (bf16[128,1024]{1,0:T(8,128)(2,1)S(1)}, bf16[128,1024]{1,0:T(8,128)(2,1)}, u32[]{:S(2)}, u32[]{:S(2)}) collective-permute-start(bf16[128,1024]{1,0:T(8,128)(2,1)S(1)} %get-tuple-element.37), channel_id=1, source_target_pairs={{1,2},{6,5},{10,9},{13,14},{17,18},{22,21},{26,25},{29,30}} | collective-permute-start | bytes 786440 | tf_op jit(solution)/shard_map/ppermute | solution.py:64
  170.4 32.5 %collective-permute-start.24 = (bf16[128,1024]{1,0:T(8,128)(2,1)S(1)}, bf16[128,1024]{1,0:T(8,128)(2,1)}, u32[]{:S(2)}, u32[]{:S(2)}) collective-permute-start(bf16[128,1024]{1,0:T(8,128)(2,1)S(1)} %get-tuple-element.37), channel_id=1, source_target_pairs={{1,0},{6,7},{10,11},{13,12},{17,16},{22,23},{26,27},{29,28}} | collective-permute-start | bytes 786440 | tf_op jit(solution)/shard_map/ppermute | solution.py:64
  171.7 31.2 %collective-permute-start.25 = (bf16[128,1024]{1,0:T(8,128)(2,1)S(1)}, bf16[128,1024]{1,0:T(8,128)(2,1)}, u32[]{:S(2)}, u32[]{:S(2)}) collective-permute-start(bf16[128,1024]{1,0:T(8,128)(2,1)S(1)} %get-tuple-element.37), channel_id=1, source_target_pairs={{1,3},{6,4},{10,8},{13,15},{17,19},{22,20},{26,24},{29,31}} | collective-permute-start | bytes 786440 | tf_op jit(solution)/shard_map/ppermute | solution.py:64
  204.9 4.6 %collective-permute-start.20 = (bf16[64,1024]{1,0:T(8,128)(2,1)S(1)}, bf16[64,1024]{1,0:T(8,128)(2,1)S(1)}, u32[]{:S(2)}, u32[]{:S(2)}) collective-permute-start(bf16[64,1024]{1,0:T(8,128)(2,1)S(1)} %get-tuple-element.64), channel_id=1, source_target_pairs={{13,10},{29,26}} | collective-permute-start | bytes 393224 | tf_op jit(solution)/shard_map/ppermute | solution.py:64
  205.6 3.9 %collective-permute-start.21 = (bf16[64,1024]{1,0:T(8,128)(2,1)S(1)}, bf16[64,1024]{1,0:T(8,128)(2,1)S(1)}, u32[]{:S(2)}, u32[]{:S(2)}) collective-permute-start(bf16[64,1024]{1,0:T(8,128)(2,1)S(1)} %get-tuple-element.63), channel_id=1, source_target_pairs={{13,26},{29,10}} | collective-permute-start | bytes 393224 | tf_op jit(solution)/shard_map/ppermute | solution.py:64
  229.5 7.9 %collective-permute-start.27 = (bf16[128,512]{1,0:T(8,128)(2,1)S(1)}, bf16[128,512]{1,0:T(8,128)(2,1)S(1)}, u32[]{:S(2)}, u32[]{:S(2)}) collective-permute-start(bf16[128,512]{1,0:T(8,128)(2,1)S(1)} %constant_dynamic-slice_fusion.3), channel_id=1, source_target_pairs={{0,16},{1,17},{2,18},{3,19},{4,20},{5,21},{6,22},{7,23},{8,24},{9,... | collective-permute-start | bytes 393224 | tf_op jit(solution)/shard_map/ppermute | solution.py:64
  231.1 6.3 %collective-permute-start.28 = (bf16[128,384]{1,0:T(8,128)(2,1)S(1)}, bf16[128,384]{1,0:T(8,128)(2,1)S(1)}, u32[]{:S(2)}, u32[]{:S(2)}) collective-permute-start(bf16[128,384]{1,0:T(8,128)(2,1)S(1)} %constant_dynamic-slice_fusion.2), channel_id=1, source_target_pairs={{0,16},{1,17},{2,18},{3,19},{4,20},{5,21},{6,22},{7,23},{8,24},{9,... | collective-permute-start | bytes 294920 | tf_op jit(solution)/shard_map/ppermute | solution.py:64
  260.2 43.1 %collective-permute-start.31 = (bf16[128,1024]{1,0:T(8,128)(2,1)S(1)}, bf16[128,1024]{1,0:T(8,128)(2,1)S(1)}, u32[]{:S(2)}, u32[]{:S(2)}) collective-permute-start(bf16[128,1024]{1,0:T(8,128)(2,1)S(1)} %maximum_select_fusion.4), channel_id=1, source_target_pairs={{1,0},{6,7},{10,11},{13,12},{17,16},{22,23},{26,27},{29,28}} | collective-permute-start | bytes 786440 | tf_op jit(solution)/shard_map/ppermute | solution.py:64
  261.5 41.8 %collective-permute-start.32 = (bf16[128,1024]{1,0:T(8,128)(2,1)S(1)}, bf16[128,1024]{1,0:T(8,128)(2,1)S(1)}, u32[]{:S(2)}, u32[]{:S(2)}) collective-permute-start(bf16[128,1024]{1,0:T(8,128)(2,1)S(1)} %maximum_select_fusion.4), channel_id=1, source_target_pairs={{1,3},{6,4},{10,8},{13,15},{17,19},{22,20},{26,24},{29,31}} | collective-permute-start | bytes 786440 | tf_op jit(solution)/shard_map/ppermute | solution.py:64
  303.4 15.0 %collective-permute-start.35 = (bf16[128,1024]{1,0:T(8,128)(2,1)S(1)}, bf16[128,1024]{1,0:T(8,128)(2,1)S(1)}, u32[]{:S(2)}, u32[]{:S(2)}) collective-permute-start(bf16[128,1024]{1,0:T(8,128)(2,1)S(1)} %add_select_fusion), channel_id=1, source_target_pairs={{0,16},{1,17},{2,18},{3,19},{4,20},{5,21},{6,22},{7,23},{8,24},{9,... | collective-permute-start | bytes 786440 | tf_op jit(solution)/shard_map/ppermute | solution.py:64
  309.8 5.7 %collective-permute-start.34 = (bf16[128,768]{1,0:T(8,128)(2,1)S(1)}, bf16[128,768]{1,0:T(8,128)(2,1)S(1)}, u32[]{:S(2)}, u32[]{:S(2)}) collective-permute-start(bf16[128,768]{1,0:T(8,128)(2,1)S(1)} %fusion.127), channel_id=1, source_target_pairs={{0,16},{1,17},{2,18},{3,19},{4,20},{5,21},{6,22},{7,23},{8,24},{9,... | collective-permute-start | bytes 589832 | tf_op jit(solution)/shard_map/ppermute | solution.py:64
  (48 other events, 543.8 us)
